TPU v7x, 32 devices: a whole 2x2x4 slice. The times are simulated.
32 devices in a mesh: section: 4 (over y, x), dp: 8 (over z, core).
Axes of the slice: x: 2, y: 2, z: 4, core: 2. Of those that a mesh axis runs over, the one named last changes fastest.
Arguments:
- latent: bfloat16 [24576, 256], P('dp'), may hold values from -6 to 6
- lengths: int32 [24576], P('dp'), may hold values from 2 to 4, as said below
- actions: int32 [5, 24576], P(None, 'dp'), may hold values from 0 to 3
- chances: int32 [4, 24576], P(None, 'dp'), may hold values from 0 to 31
- value_bins: int32 [4, 24576], P(None, 'dp'), may hold values from 0 to 600
- reward_bins: int32 [4, 24576], P(None, 'dp'), may hold values from 0 to 600
- entry_w: bfloat16 [4, 2, 256, 256], P('section'), may hold values from -0.375 to 0.375
- action_w: bfloat16 [4, 4, 256], P('section'), may hold values from -6 to 6
- chance_w: bfloat16 [4, 32, 256], P('section'), may hold values from -6 to 6
- block_w: bfloat16 [4, 2, 2, 2, 256, 256], P('section'), may hold values from -0.375 to 0.375
- gain_w: bfloat16 [4, 2, 5, 256], P('section'), may hold values from 0.5 to 1.5
- shift_w: bfloat16 [4, 2, 5, 256], P('section'), may hold values from -1.5 to 1.5
- state_head: bfloat16 [256, 1206], replicated, may hold values from -1.5 to 1.5
- chance_head: bfloat16 [256, 32], replicated, may hold values from -1.5 to 1.5
Outputs:
- latent_grad: float32 [6144, 4, 256], P('dp', 'section')
- entry_grad: float32 [4, 2, 256, 256], P('section')
- action_grad: float32 [4, 4, 256], P('section')
- chance_grad: float32 [4, 32, 256], P('section')
- block_grad: float32 [4, 2, 2, 2, 256, 256], P('section')
- gain_grad: float32 [4, 2, 5, 256], P('section')
- shift_grad: float32 [4, 2, 5, 256], P('section')
- state_head_grad: float32 [256, 1206], replicated
- chance_head_grad: float32 [256, 32], replicated
- loss: float32 [], replicated
Inputs may be any that keep to these rules, and one draw needn't show every extreme that they name: `lengths`: every state unrolls either half of 4 steps or all 4.
All inputs are finite; a program needn't handle non-finite values.
Results may differ from a plain program's by a relative error of at most 0.02.
Values may be sent and summed in bfloat16 or wider, within the bound.
A program may use at most 192 MiB of HBM per device.

v0:
```python
import jax
import jax.numpy as jnp
from jax import lax
from jax.sharding import PartitionSpec as P

MICRO = 8


NORM_EPS = 1e-05
HALF_SCALE = 0.5


def as_sent(shard):

    def short(part):
        return part.astype(jnp.bfloat16) if part.dtype == jnp.float32 else part

    return jax.tree.map(short, shard)


def layer_norm(values):
    center = values - jnp.mean(values, axis=-1, keepdims=True)
    spread = jnp.mean(center * center, axis=-1, keepdims=True)
    return center * lax.rsqrt(spread + NORM_EPS)


def norm_act(values, gain_vec, shift_vec):
    return jax.nn.gelu(layer_norm(values) * gain_vec + shift_vec)


def block_out(residual, branch, gain_vec, shift_vec):
    return jax.nn.gelu(residual + layer_norm(branch) * gain_vec + shift_vec)


def product(left_mat, right_mat):
    return jnp.dot(left_mat, right_mat, preferred_element_type=jnp.float32)


def product_tn(left_mat, right_mat):
    return lax.dot_general(
        left_mat, right_mat, (((0,), (0,)), ((), ())), preferred_element_type=jnp.float32
    )


def product_nt(left_mat, right_mat):
    return lax.dot_general(
        left_mat, right_mat, (((1,), (1,)), ((), ())), preferred_element_type=jnp.float32
    )


def tower_forward(state_low, picked, params):
    entry_mat, lookup, blocks, gain_rows, shifts = params
    first_sum = product(state_low, entry_mat) + product(picked, lookup)
    latent_state = norm_act(first_sum, gain_rows[0], shifts[0])
    inputs, hidden, inner_low, second = ([], [], [], [])
    for block_at in range(blocks.shape[0]):
        inputs.append(latent_state)
        pre_act = product(latent_state.astype(jnp.bfloat16), blocks[block_at, 0])
        mid_low = norm_act(pre_act, gain_rows[1 + 2 * block_at], shifts[1 + 2 * block_at]).astype(
            jnp.bfloat16
        )
        post_act = product(mid_low, blocks[block_at, 1])
        hidden.append(pre_act)
        inner_low.append(mid_low)
        second.append(post_act)
        latent_state = block_out(
            latent_state, post_act, gain_rows[2 + 2 * block_at], shifts[2 + 2 * block_at]
        )
    return (latent_state, (first_sum, inputs, hidden, inner_low, second))


def tower_backward(state_low, picked, params, cached, gradient):
    entry_mat, lookup, blocks, gain_rows, shifts = params
    first_sum, inputs, hidden, inner_low, second = cached
    block_count = blocks.shape[0]
    gain_grads = [None] * (1 + 2 * block_count)
    shift_grads = [None] * (1 + 2 * block_count)
    weight_grads = [None] * block_count
    for block_at in reversed(range(block_count)):
        inner_at = 1 + 2 * block_at
        outer_at = 2 + 2 * block_at
        unused_out, pullback = jax.vjp(
            block_out, inputs[block_at], second[block_at], gain_rows[outer_at], shifts[outer_at]
        )
        d_resid, d_post, gain_grads[outer_at], shift_grads[outer_at] = pullback(gradient)
        d_post = d_post.astype(jnp.bfloat16)
        w_out = product_tn(inner_low[block_at], d_post)
        d_mid = product_nt(d_post, blocks[block_at, 1])
        unused_out, pullback = jax.vjp(
            norm_act, hidden[block_at], gain_rows[inner_at], shifts[inner_at]
        )
        d_pre, gain_grads[inner_at], shift_grads[inner_at] = pullback(d_mid)
        d_pre = d_pre.astype(jnp.bfloat16)
        w_in = product_tn(inputs[block_at].astype(jnp.bfloat16), d_pre)
        gradient = d_resid + product_nt(d_pre, blocks[block_at, 0])
        weight_grads[block_at] = jnp.stack([w_in, w_out])
    unused_out, pullback = jax.vjp(norm_act, first_sum, gain_rows[0], shifts[0])
    d_first, gain_grads[0], shift_grads[0] = pullback(gradient)
    d_first = d_first.astype(jnp.bfloat16)
    tower_grads = (
        product_tn(state_low, d_first),
        product_tn(picked, d_first),
        jnp.stack(weight_grads),
        jnp.stack(gain_grads),
        jnp.stack(shift_grads),
    )
    return (product_nt(d_first, entry_mat), tower_grads)


def soft_loss(logits, target, live_rows):
    row_max = jnp.max(logits, axis=1, keepdims=True)
    shifted = logits - row_max
    expo_vals = jnp.exp(shifted)
    row_total = jnp.sum(expo_vals, axis=1, keepdims=True)
    picked = jax.nn.one_hot(target, logits.shape[1], dtype=jnp.float32)
    losses = jnp.log(row_total[:, 0]) - jnp.sum(shifted * picked, axis=1)
    gradient = live_rows[:, None] * (expo_vals / row_total - picked)
    return (jnp.sum(live_rows * losses), gradient)


def section_towers(entry_w, action_w, chance_w, block_w, gain_w, shift_w, step_at):
    gain_rows = gain_w[step_at].astype(jnp.float32)
    shifts = shift_w[step_at].astype(jnp.float32)
    tower_one = (
        entry_w[step_at, 0],
        action_w[step_at],
        block_w[step_at, 0],
        gain_rows[0],
        shifts[0],
    )
    tower_two = (
        entry_w[step_at, 1],
        chance_w[step_at],
        block_w[step_at, 1],
        gain_rows[1],
        shifts[1],
    )
    return (tower_one, tower_two)


def step_forward(state_low, targets, tower_one, tower_two, state_head, chance_head, live_rows):
    act_now, act_next, chance_now, value_now, reward_now = targets
    pick_action = jax.nn.one_hot(act_now, tower_one[1].shape[0], dtype=jnp.bfloat16)
    pick_chance = jax.nn.one_hot(chance_now, tower_two[1].shape[0], dtype=jnp.bfloat16)
    after_state, cached_one = tower_forward(state_low, pick_action, tower_one)
    after_low = after_state.astype(jnp.bfloat16)
    chance_logits = product(after_low, chance_head)
    next_state, cached_two = tower_forward(after_low, pick_chance, tower_two)
    next_low = next_state.astype(jnp.bfloat16)
    logits = product(next_low, state_head)
    bin_count = (logits.shape[1] - pick_action.shape[1]) // 2
    loss_value, grad_value = soft_loss(logits[:, :bin_count], value_now, live_rows)
    loss_reward, grad_reward = soft_loss(
        logits[:, bin_count : 2 * bin_count], reward_now, live_rows
    )
    loss_policy, grad_policy = soft_loss(logits[:, 2 * bin_count :], act_next, live_rows)
    loss_chance, grad_chance = soft_loss(chance_logits, chance_now, live_rows)
    d_state = jnp.concatenate([grad_value, grad_reward, grad_policy], axis=1).astype(jnp.bfloat16)
    cached = (
        state_low,
        pick_action,
        cached_one,
        after_low,
        pick_chance,
        cached_two,
        next_low,
        d_state,
        grad_chance.astype(jnp.bfloat16),
    )
    return (next_low, loss_value + loss_reward + loss_policy + loss_chance, cached)


def step_backward(cached, cotangent, weight, tower_one, tower_two, state_head, chance_head):
    (
        state_low,
        pick_action,
        cached_one,
        after_low,
        pick_chance,
        cached_two,
        next_low,
        d_state,
        d_chance,
    ) = cached
    d_state = d_state * weight
    d_chance = d_chance * weight
    head_step = product_tn(next_low, d_state)
    chance_step = product_tn(after_low, d_chance)
    grad_next = cotangent + product_nt(d_state, state_head)
    d_after, grads_two = tower_backward(after_low, pick_chance, tower_two, cached_two, grad_next)
    grad_after = d_after + product_nt(d_chance, chance_head)
    d_input, grads_one = tower_backward(state_low, pick_action, tower_one, cached_one, grad_after)
    section_grads = (
        jnp.stack([grads_one[0], grads_two[0]]),
        grads_one[1],
        grads_two[1],
        jnp.stack([grads_one[2], grads_two[2]]),
        jnp.stack([grads_one[3], grads_two[3]]),
        jnp.stack([grads_one[4], grads_two[4]]),
    )
    return (d_input, section_grads, head_step, chance_step)


def per_device(
    latent,
    lengths,
    actions,
    chances,
    value_bins,
    reward_bins,
    entry_w,
    action_w,
    chance_w,
    block_w,
    gain_w,
    shift_w,
    state_head,
    chance_head,
):
    section_index = lax.axis_index("section")
    section_count = lax.axis_size("section")
    row_count, feature_count = latent.shape
    block_rows = row_count // MICRO
    quarter_rows = row_count // section_count
    tower_args = (entry_w, action_w, chance_w, block_w, gain_w, shift_w)
    head_zero = jnp.zeros(state_head.shape, jnp.float32)
    chance_zero = jnp.zeros(chance_head.shape, jnp.float32)
    full_towers = (
        lax.all_gather(tower_args[0], "section", axis=0, tiled=True),
        lax.all_gather(tower_args[1], "section", axis=0, tiled=True),
        lax.all_gather(tower_args[2], "section", axis=0, tiled=True),
        lax.all_gather(tower_args[3], "section", axis=0, tiled=True),
        lax.all_gather(tower_args[4], "section", axis=0, tiled=True),
        lax.all_gather(tower_args[5], "section", axis=0, tiled=True),
    )
    towers = [section_towers(*full_towers, step_at) for step_at in range(section_count)]

    def own_rows(source):
        shaped = source.reshape(source.shape[:-1] + (quarter_rows, section_count))
        return lax.dynamic_index_in_dim(shaped, section_index, shaped.ndim - 1, keepdims=False)

    latent_own = lax.dynamic_index_in_dim(
        latent.reshape(quarter_rows, section_count, feature_count), section_index, 1, keepdims=False
    )
    lengths_own = own_rows(lengths)
    actions_own = own_rows(actions)
    chances_own = own_rows(chances)
    values_own = own_rows(value_bins)
    rewards_own = own_rows(reward_bins)
    group_total = quarter_rows // block_rows

    def group_pass(carry, group_at):
        grad_sum, head_sum, chance_sum, loss_sum = carry
        row_start = group_at * block_rows

        def slice_rows(source):
            return lax.dynamic_slice_in_dim(source, row_start, block_rows, source.ndim - 1)

        act_rows = slice_rows(actions_own)
        chance_rows = slice_rows(chances_own)
        value_rows = slice_rows(values_own)
        reward_rows = slice_rows(rewards_own)
        length_rows = slice_rows(lengths_own)

        def targets_at(step_at):
            return (
                act_rows[step_at],
                act_rows[step_at + 1],
                chance_rows[step_at],
                value_rows[step_at],
                reward_rows[step_at],
            )

        current = lax.dynamic_slice_in_dim(latent_own, row_start, block_rows, 0)
        stored = []
        for step_at in range(section_count):
            live_rows = (length_rows > step_at).astype(jnp.float32)
            next_low, loss_step, cached = step_forward(
                current,
                targets_at(step_at),
                towers[step_at][0],
                towers[step_at][1],
                state_head,
                chance_head,
                live_rows,
            )
            loss_sum = loss_sum + loss_step
            stored.append(current)
            current = next_low
        cotangent = jnp.zeros((block_rows, feature_count), jnp.float32)
        step_grads = [None] * section_count
        d_input = cotangent
        for step_at in reversed(range(section_count)):
            live_rows = (length_rows > step_at).astype(jnp.float32)
            unused_next, unused_loss, cached = step_forward(
                stored[step_at],
                targets_at(step_at),
                towers[step_at][0],
                towers[step_at][1],
                state_head,
                chance_head,
                live_rows,
            )
            d_input, step_grads[step_at], head_step, chance_step = step_backward(
                cached,
                cotangent,
                jnp.bfloat16(1.0),
                towers[step_at][0],
                towers[step_at][1],
                state_head,
                chance_head,
            )
            head_sum = head_sum + head_step
            chance_sum = chance_sum + chance_step
            cotangent = (HALF_SCALE * d_input).astype(jnp.bfloat16).astype(jnp.float32)
        stacked = jax.tree.map(lambda *pieces: jnp.stack(pieces), *step_grads)
        grad_sum = jax.tree.map(jnp.add, grad_sum, stacked)
        return ((grad_sum, head_sum, chance_sum, loss_sum), HALF_SCALE * d_input)

    grad_zero = tuple((jnp.zeros(source.shape, jnp.float32) for source in full_towers))
    start_carry = (grad_zero, head_zero, chance_zero, jnp.float32(0.0))
    (grad_sum, head_grad, chance_head_grad, loss_sum), first_all = lax.scan(
        group_pass, start_carry, jnp.arange(group_total)
    )
    latent_grad = first_all.reshape(quarter_rows, 1, feature_count)
    tower_grads = jax.tree.map(
        lambda part: part.astype(jnp.float32),
        lax.psum_scatter(as_sent(grad_sum), "section", scatter_dimension=0, tiled=True),
    )
    tower_grads = lax.psum(tower_grads, "dp")
    head_grad, chance_head_grad, loss_sum = lax.psum(
        (head_grad, chance_head_grad, loss_sum), ("section", "dp")
    )
    scale = 1.0 / (row_count * lax.axis_size("dp"))
    entry_grad, action_grad, chance_grad, block_grad, gain_grad, shift_grad = tuple(
        (source * scale for source in tower_grads)
    )
    return (
        latent_grad,
        entry_grad,
        action_grad,
        chance_grad,
        block_grad,
        gain_grad,
        shift_grad,
        head_grad * scale,
        chance_head_grad * scale,
        loss_sum * scale,
    )


def solution(mesh):
    placed = (
        P("dp", None),
        P("dp"),
        P(None, "dp"),
        P(None, "dp"),
        P(None, "dp"),
        P(None, "dp"),
        P("section", None, None, None),
        P("section", None, None),
        P("section", None, None),
        P("section", None, None, None, None, None),
        P("section", None, None, None),
        P("section", None, None, None),
        P(),
        P(),
    )
    return jax.shard_map(
        per_device,
        mesh=mesh,
        in_specs=placed,
        out_specs=(
            P("dp", "section", None),
            P("section", None, None, None),
            P("section", None, None),
            P("section", None, None),
            P("section", None, None, None, None, None),
            P("section", None, None, None),
            P("section", None, None, None),
            P(),
            P(),
            P(),
        ),
        check_vma=False,
    )
```

profile of v0, /device:TPU:0, one launch (start us, length us, event | category | flops | bytes accessed | tf_op | source)
XLA Modules:
  0.0 1315.3 jit_solution(11372813984411535635)
XLA Ops:
  8.8 9.7 all_gather.21
  23.4 8.0 all_gather.20
  40.7 2.8 reshape.1596
  43.5 2.8 reshape.1597
  46.3 2.8 reshape.1598
  51.2 7.2 all_gather.19
  59.3 8.3 all_gather.23
  67.7 2.9 dynamic-slice_reduce_fusion.20
  78.2 16.0 %all-gather.5.cloned.1.call-done = bf16[4,2,2,2,256,256]{5,4,3,2,1,0:T(8,128)(2,1)} async-done(((bf16[1,2,2,2,256,256]{5,4,3,2,1,0:T(8,128)(2,1)}), bf16[4,2,2,2,256,256]{5,4,3,2,1,0:T(8,128)(2,1)}) %all-gather.5.cloned.1.call-update) | async-done | bytes 4194320 | tf_op jit(solution)/shard_map/all_gather | solution.py:232
  94.2 4.2 slice_bitcast_fusion
  98.9 888.7 %while.32 = (s32[]{:T(128)}, f32[4,2,256,256]{3,2,1,0:T(8,128)}, f32[4,4,256]{2,1,0:T(4,128)}, f32[4,32,256]{2,1,0:T(8,128)}, f32[4,2,2,2,256,256]{5,4,3,2,1,0:T...) while((s32[]{:T(128)}, f32[4,2,256,256]{3,2,1,0:T(8,128)}, ...), condition=%wide.region_305.306_spmd.clone, body=%wide.region_0.305_spmd.clone.sunk | while | flops 9349187584 | bytes 701252480 | solution.py:322
  261.5 7.8 concatenate.40
  273.7 8.3 concatenate.42
  357.8 5.0 concatenate.41
  362.9 2.7 multiply_reduce_fusion.250
  374.0 7.2 concatenate.43
  381.3 2.8 convolution_add_fusion.50
  522.9 4.1 maximum_add_fusion.14
  702.4 7.8 concatenate.40
  714.5 8.3 concatenate.42
  798.6 5.0 concatenate.41
  803.7 2.7 multiply_reduce_fusion.250
  814.8 7.2 concatenate.43
  822.1 2.8 convolution_add_fusion.50
  963.7 6.3 maximum_add_fusion.14
  992.6 6.0 convert_element_type.969
  1002.3 40.5 %all-reduce.6 = (f32[256,32]{0,1:T(8,128)S(1)}, f32[]{:T(128)}) all-reduce(f32[256,32]{0,1:T(8,128)S(1)} %copy-done.504, f32[]{:T(128)} %get-tuple-element.917), channel_id=1, replica_groups=mesh['section'=4,'dp'=8] {'section','dp'}, use_global_device_ids=true, to_apply=%region_319.320 | all-reduce | flops 8193 | bytes 65544 | tf_op jit(solution)/shard_map/psum | solution.py:331
  1043.4 17.5 %all-reduce.8 = (bf16[4,4,256]{2,1,0:T(4,128)(2,1)S(1)}, bf16[4,2,5,256]{3,1,2,0:T(2,128)(2,1)S(1)}, bf16[4,2,5,256]{3,1,2,0:T(2,128)(2,1)S(1)}) all-reduce(bf16[4,4,256]{2,1,0:T(4,128)(2,1)S(1)} %convert_element_type.965, bf16[4,2,5,256]{3,1,2,0:T(2,128)(2,1)S(1)} %copy.398, ...), channel_id=3, replica_groups=mesh['section'=4,'dp'=8] {'section'}, use_global_device_ids=true, to_apply=%region_308.309.clone | all-reduce | flops 24576 | bytes 98304
  1063.5 86.8 %all-reduce.12.cloned.1.call-done = f32[256,1206]{0,1:T(8,128)} async-done(((f32[256,1206]{0,1:T(8,128)}), f32[256,1206]{0,1:T(8,128)}) %all-reduce.12.cloned.1.call-update) | async-done | bytes 1234960 | tf_op jit(solution)/shard_map/psum | solution.py:331
  1152.8 28.1 %reduce-scatter.10.cloned.1.call-done = bf16[1,2,256,256]{3,2,1,0:T(8,128)(2,1)} async-done(((bf16[4,2,256,256]{3,2,1,0:T(8,128)(2,1)}), bf16[1,2,256,256]{3,2,1,0:T(8,128)(2,1)}) %reduce-scatter.10.cloned.1.call-update) | async-done | bytes 262160
  1180.9 55.5 %reduce-scatter.14.cloned.1.call-done = bf16[1,2,2,2,256,256]{5,4,3,2,1,0:T(8,128)(2,1)} async-done(((bf16[4,2,2,2,256,256]{5,4,3,2,1,0:T(8,128)(2,1)}), bf16[1,2,2,2,256,256]{5,4,3,2,1,0:T(8,128)(2,1)}) %reduce-scatter.14.cloned.1.call-update) | async-done | bytes 1048592
  1236.4 65.9 %all-reduce.13 = (f32[1,2,256,256]{3,2,1,0:T(8,128)S(1)}, f32[1,4,256]{2,1,0:T(4,128)S(1)}, f32[1,32,256]{2,1,0:T(8,128)S(1)}, f32[1,2,2,2,256,256]{5,4,3,2,1,0:...) all-reduce(bf16[1,2,256,256]{3,2,1,0:T(8,128)(2,1)} %reduce-scatter, ...), channel_id=1, replica_groups=mesh['section'=4,'dp'=8] {'dp'}, use_global_device_ids=true, to_apply=%region_307.308 | all-reduce | flops 669696 | bytes 4030464 | tf_op jit(solution)/shard_map/psum | solution.py:330
  (3263 shorter events, 813.2 us)
Async XLA Ops:
  7.2 29.1 %copy-start.536 = (s32[3072]{0:T(1024)S(1)}, s32[3072]{0:T(1024)}, u32[]{:S(2)}) copy-start(s32[3072]{0:T(1024)} %param.17) | copy-start | bytes 36868
  7.2 68.7 %all-gather.3.cloned.1.call-start = ((), (), s32[]{:S(2)}) async-start(), calls=%async_computation.3 | async-start | bytes 1310720 | tf_op jit(solution)/shard_map/all_gather | solution.py:229
  7.9 86.2 %all-gather.5.cloned.1.call-start = ((), (), s32[]{:S(2)}) async-start(), calls=%async_computation.4 | async-start | bytes 5242880 | tf_op jit(solution)/shard_map/all_gather | solution.py:232
  8.7 1054.9 %reduce-scatter.12.cloned.1.call-start = ((), (), s32[]{:S(2)}) async-start(), calls=%async_computation.7 | async-start | bytes 81920
  78.2 20.7 %copy-start.6 = (bf16[256,1206]{0,1:T(8,128)(2,1)S(1)}, bf16[256,1206]{0,1:T(8,128)(2,1)}, u32[]{:S(2)}) copy-start(bf16[256,1206]{0,1:T(8,128)(2,1)} %param.28) | copy-start | bytes 1852420
  78.2 20.7 %copy-start.133 = (bf16[256,32]{0,1:T(8,128)(2,1)S(1)}, bf16[256,32]{0,1:T(8,128)(2,1)}, u32[]{:S(2)}) copy-start(bf16[256,32]{0,1:T(8,128)(2,1)} %param.29) | copy-start | bytes 49156
  121.9 27.8 %copy-start.437 = (f32[1,256]{1,0:T(1,128)}, f32[1,256]{1,0:T(1,128)S(1)}, u32[]{:S(2)}) copy-start(f32[1,256]{1,0:T(1,128)S(1)} %get-tuple-element.2726) | copy-start | bytes 3076 | tf_op jit(solution)/shard_map/while
  121.9 27.8 %copy-start.445 = (f32[1,256]{1,0:T(1,128)}, f32[1,256]{1,0:T(1,128)S(1)}, u32[]{:S(2)}) copy-start(f32[1,256]{1,0:T(1,128)S(1)} %get-tuple-element.2758) | copy-start | bytes 3076 | tf_op jit(solution)/shard_map/while
  122.8 16.3 %copy-start.507 = (f32[1,256]{1,0:T(1,128)}, f32[1,256]{1,0:T(1,128)S(1)}, u32[]{:S(2)}) copy-start(f32[1,256]{1,0:T(1,128)S(1)} %get-tuple-element.2743) | copy-start | bytes 3076 | tf_op jit(solution)/shard_map/while
  123.7 16.9 %copy-start.447 = (f32[1,256]{1,0:T(1,128)}, f32[1,256]{1,0:T(1,128)S(1)}, u32[]{:S(2)}) copy-start(f32[1,256]{1,0:T(1,128)S(1)} %get-tuple-element.2728) | copy-start | bytes 3076 | tf_op jit(solution)/shard_map/while
  128.3 72.7 %copy-start.173 = (s32[384]{0:T(512)}, s32[384]{0:T(512)S(1)}, u32[]{:S(2)}) copy-start(s32[384]{0:T(512)S(1)} %get-tuple-element.2822) | copy-start | bytes 4612 | tf_op jit(solution)/shard_map/while
  129.9 27.9 %copy-start.176 = (s32[384]{0:T(512)}, s32[384]{0:T(512)S(1)}, u32[]{:S(2)}) copy-start(s32[384]{0:T(512)S(1)} %get-tuple-element.2767) | copy-start | bytes 4612 | tf_op jit(solution)/shard_map/while
  185.4 62.0 %copy-start.23 = (bf16[384,256]{0,1:T(8,128)(2,1)}, bf16[384,256]{0,1:T(8,128)(2,1)S(1)}, u32[]{:S(2)}) copy-start(bf16[384,256]{0,1:T(8,128)(2,1)S(1)} %get-tuple-element.2802) | copy-start | bytes 589828 | tf_op jit(solution)/shard_map/while
  199.2 170.9 %copy-start.137 = (f32[384,32]{0,1:T(8,128)}, f32[384,32]{0,1:T(8,128)S(1)}, u32[]{:S(2)}) copy-start(f32[384,32]{0,1:T(8,128)S(1)} %get-tuple-element.2982) | copy-start | bytes 147460 | tf_op jit(solution)/shard_map/while
  212.9 30.7 %copy-start.25 = (bf16[384,256]{0,1:T(8,128)(2,1)}, bf16[384,256]{0,1:T(8,128)(2,1)S(1)}, u32[]{:S(2)}) copy-start(bf16[384,256]{0,1:T(8,128)(2,1)S(1)} %get-tuple-element.2844) | copy-start | bytes 589828 | tf_op jit(solution)/shard_map/while
  215.2 118.7 %copy-start.168 = (f32[384]{0:T(512)}, f32[384]{0:T(512)S(1)}, u32[]{:S(2)}) copy-start(f32[384]{0:T(512)S(1)} %broadcast_multiply_fusion.118) | copy-start | bytes 4612 | tf_op jit(solution)/shard_map/while
  562.6 27.9 %copy-start.437 = (f32[1,256]{1,0:T(1,128)}, f32[1,256]{1,0:T(1,128)S(1)}, u32[]{:S(2)}) copy-start(f32[1,256]{1,0:T(1,128)S(1)} %get-tuple-element.2726) | copy-start | bytes 3076 | tf_op jit(solution)/shard_map/while
  562.6 27.9 %copy-start.445 = (f32[1,256]{1,0:T(1,128)}, f32[1,256]{1,0:T(1,128)S(1)}, u32[]{:S(2)}) copy-start(f32[1,256]{1,0:T(1,128)S(1)} %get-tuple-element.2758) | copy-start | bytes 3076 | tf_op jit(solution)/shard_map/while
  563.5 16.4 %copy-start.507 = (f32[1,256]{1,0:T(1,128)}, f32[1,256]{1,0:T(1,128)S(1)}, u32[]{:S(2)}) copy-start(f32[1,256]{1,0:T(1,128)S(1)} %get-tuple-element.2743) | copy-start | bytes 3076 | tf_op jit(solution)/shard_map/while
  564.4 15.5 %copy-start.495 = (f32[1,256]{1,0:T(1,128)}, f32[1,256]{1,0:T(1,128)S(1)}, u32[]{:S(2)}) copy-start(f32[1,256]{1,0:T(1,128)S(1)} %get-tuple-element.2744) | copy-start | bytes 3076 | tf_op jit(solution)/shard_map/while
  564.4 17.0 %copy-start.447 = (f32[1,256]{1,0:T(1,128)}, f32[1,256]{1,0:T(1,128)S(1)}, u32[]{:S(2)}) copy-start(f32[1,256]{1,0:T(1,128)S(1)} %get-tuple-element.2728) | copy-start | bytes 3076 | tf_op jit(solution)/shard_map/while
  569.0 15.5 %copy-start.170 = (s32[384]{0:T(512)}, s32[384]{0:T(512)S(1)}, u32[]{:S(2)}) copy-start(s32[384]{0:T(512)S(1)} %get-tuple-element.2749) | copy-start | bytes 4612 | tf_op jit(solution)/shard_map/while
  569.0 72.8 %copy-start.173 = (s32[384]{0:T(512)}, s32[384]{0:T(512)S(1)}, u32[]{:S(2)}) copy-start(s32[384]{0:T(512)S(1)} %get-tuple-element.2822) | copy-start | bytes 4612 | tf_op jit(solution)/shard_map/while
  570.8 27.9 %copy-start.176 = (s32[384]{0:T(512)}, s32[384]{0:T(512)S(1)}, u32[]{:S(2)}) copy-start(s32[384]{0:T(512)S(1)} %get-tuple-element.2767) | copy-start | bytes 4612 | tf_op jit(solution)/shard_map/while
  626.2 62.0 %copy-start.23 = (bf16[384,256]{0,1:T(8,128)(2,1)}, bf16[384,256]{0,1:T(8,128)(2,1)S(1)}, u32[]{:S(2)}) copy-start(bf16[384,256]{0,1:T(8,128)(2,1)S(1)} %get-tuple-element.2802) | copy-start | bytes 589828 | tf_op jit(solution)/shard_map/while
  640.0 170.9 %copy-start.137 = (f32[384,32]{0,1:T(8,128)}, f32[384,32]{0,1:T(8,128)S(1)}, u32[]{:S(2)}) copy-start(f32[384,32]{0,1:T(8,128)S(1)} %get-tuple-element.2982) | copy-start | bytes 147460 | tf_op jit(solution)/shard_map/while
  653.8 30.7 %copy-start.25 = (bf16[384,256]{0,1:T(8,128)(2,1)}, bf16[384,256]{0,1:T(8,128)(2,1)S(1)}, u32[]{:S(2)}) copy-start(bf16[384,256]{0,1:T(8,128)(2,1)S(1)} %get-tuple-element.2844) | copy-start | bytes 589828 | tf_op jit(solution)/shard_map/while
  656.1 118.7 %copy-start.168 = (f32[384]{0:T(512)}, f32[384]{0:T(512)S(1)}, u32[]{:S(2)}) copy-start(f32[384]{0:T(512)S(1)} %broadcast_multiply_fusion.118) | copy-start | bytes 4612 | tf_op jit(solution)/shard_map/while
  989.2 161.2 %all-reduce.12.cloned.1.call-start = ((), (), s32[]{:S(2)}) async-start(), calls=%async_computation.5 | async-start | bytes 2473984 | tf_op jit(solution)/shard_map/psum | solution.py:331
  989.8 191.1 %reduce-scatter.10.cloned.1.call-start = ((), (), s32[]{:S(2)}) async-start(), calls=%async_computation.6 | async-start | bytes 1310720
  992.5 243.9 %reduce-scatter.14.cloned.1.call-start = ((), (), s32[]{:S(2)}) async-start(), calls=%async_computation.8 | async-start | bytes 5242880
  1063.5 172.9 %copy-start.534 = (bf16[1,32,256]{2,1,0:T(8,128)(2,1)S(1)}, bf16[1,32,256]{2,1,0:T(8,128)(2,1)}, u32[]{:S(2)}) copy-start(bf16[1,32,256]{2,1,0:T(8,128)(2,1)} %reduce-scatter.12.cloned.1.call-done) | copy-start | bytes 49156
  (1039 other events, 3500.7 us)
Sparse Core Ops, SparseCore 0:
  9.9 29.3 all-gather.2
  41.1 53.0 all-gather.4
  989.3 23.6 reduce-scatter.11
  1019.8 130.5 all-reduce.11
  1153.3 27.4 reduce-scatter.9
  1183.7 52.6 reduce-scatter.13
where the time goes:
time: 1340 us; the launch traced here: 1320 us
  matrix products  423 us (32%)
  other arithmetic  255 us (19%)
  local copies, waits for them, and re-layouts  233 us (17%)
  waiting for transfers between devices  188 us (14%)
  blocking collectives  157 us (12%)
  loops' own time  42.4 us (3%)
  between operations  16.4 us (1%)
    dot_general x96, matrix products, product_nt(): lax.dot_general(left_mat, right_mat, (((1,), (1,)), ((), ())), preferred_...  185 us
    dot_general x112, matrix products, product(): return jnp.dot(left_mat, right_mat, preferred_element_type=jnp.float32)  129 us
    dot_general x112, matrix products, product_tn(): lax.dot_general(left_mat, right_mat, (((0,), (0,)), ((), ())), preferred_...  109 us
    psum x1, waiting for transfers between devices, per_device(): lax.psum((head_grad, chance_head_grad, loss_sum), ('section', 'dp'))  86.8 us
    unnamed x9, waiting for transfers between devices  85.6 us
    psum x1, blocking collectives, per_device(): tower_grads = lax.psum(tower_grads, 'dp')  65.9 us
    concatenate x8, local copies, waits for them, and re-layouts, step_forward(): jnp.concatenate([grad_value, grad_reward, grad_policy], axis=1)  56.7 us
    while x2096, local copies, waits for them, and re-layouts  55.9 us
  transfers between devices with their start and end apart: 6, of which 4 were waited for; matrix products, arithmetic and copies ran while one was open for 4% of the time, Pallas kernels for 0%

commit v1 on v0

v1 whole, which is shorter than its diff:
```python
import jax
import jax.numpy as jnp
from jax import lax
from jax.experimental import pallas as pl
from jax.experimental.pallas import tpu as pltpu
from jax.sharding import PartitionSpec as P

F32 = jnp.float32
BF16 = jnp.bfloat16
ROOT = 0.7978845608028654
K1 = 2.0 * ROOT
K2 = 8.0 * ROOT * 0.044715
EPS = 1e-05
WIDE = 256
LANES = 128
NORMS = 5
ACT_ROW = 32
GAIN_ROW = 36
SHIFT_ROW = 46
MISC_ROWS = 64


def contract(left, right, left_dim, right_dim):
    return lax.dot_general(
        left, right, (((left_dim,), (right_dim,)), ((), ())), preferred_element_type=F32
    )


def gelu_pair(half):
    square = half * half * K2
    inner = half * (square + K1)
    plus = jnp.tanh(inner) + 1.0
    slope = half * (square * 3.0 + K1)
    return half * plus, plus * ((2.0 - plus) * slope + 1.0)


def norm_forward(values, gain, shift, residual):
    feature_count = values.shape[0]
    center = values - jnp.sum(values, axis=0, keepdims=True) * (1.0 / feature_count)
    inverse = lax.rsqrt(jnp.sum(center * center, axis=0, keepdims=True) + feature_count * EPS)
    unit = center * inverse
    half = unit * gain + shift
    if residual is not None:
        half = half + 0.5 * residual
    out, slope = gelu_pair(half)
    return out, slope, unit, inverse


def kernel(
    latent, lengths, actions, chances, values, rewards, entry, blocks, action_w, chance_w, gains, shifts,
    state_head, chance_head,
    latent_out, tower_out, misc_out, head_out, loss_out, spill,
    weights, misc, head, acts, inv, ids, onehot, current, resid, prod_a, prod_b, grad, gb, acc_dy, acc_p,
    logits, dlogits, dchance, head_back, head_sum, misc_grad, sel, stage,
    w_sem, spill_sem,
):
    section = lax.axis_index("section")
    rows = current.shape[1]
    steps = weights.shape[0]
    feat = WIDE
    head_width = state_head.shape[1]
    bins = (head_width - action_w.shape[1]) // 2
    head_pad = head.shape[1]
    action_count = action_w.shape[1]
    chunks = [slice(c, c + WIDE) for c in range(0, rows, WIDE)]

    def subs(part):
        return [slice(c, c + LANES) for c in range(part.start, part.stop, LANES)]

    copies = []
    for k in range(steps):
        for t in range(2):
            copies.append((entry.at[k, t], weights.at[k, 5 * t]))
            for j in range(2):
                for i in range(2):
                    copies.append((blocks.at[k, t, j, i], weights.at[k, 5 * t + 1 + 2 * j + i]))
    for n, (src, dst) in enumerate(copies):
        pltpu.make_async_copy(src, dst, w_sem.at[n]).start()

    for k in range(steps):
        packed = jnp.concatenate(
            [
                chance_w[k].astype(F32),
                action_w[k].astype(F32),
                gains[k].astype(F32),
                shifts[k].astype(F32),
                jnp.zeros((MISC_ROWS - SHIFT_ROW - 2 * NORMS, feat), F32),
            ],
            axis=0,
        )
        misc[k] = packed.astype(BF16)
    head[...] = jnp.zeros_like(head)
    head[:, 0:head_width] = state_head[...]

    steps_of = steps
    pick_at = lax.broadcasted_iota(jnp.int32, (steps_of * WIDE, WIDE), 0)
    pick_to = lax.broadcasted_iota(jnp.int32, (steps_of * WIDE, WIDE), 1)
    sel[...] = (pick_at == steps_of * pick_to + section).astype(F32).astype(BF16)
    stage[...] = jnp.zeros_like(stage)
    stage[0:1] = lengths[...].astype(F32)
    stage[1:6] = actions[...].astype(F32)
    stage[6:10] = chances[...].astype(F32)
    stage[10:14] = lax.shift_right_logical(values[...], 5).astype(F32)
    stage[14:18] = (values[...] & 31).astype(F32)
    stage[18:22] = lax.shift_right_logical(rewards[...], 5).astype(F32)
    stage[22:26] = (rewards[...] & 31).astype(F32)
    for n, part in enumerate(chunks):
        rows_in = slice(n * steps_of * WIDE, (n + 1) * steps_of * WIDE)
        current[:, part] = contract(latent[rows_in], sel[...], 0, 0).astype(BF16)
        got = contract(stage[:, rows_in].astype(BF16), sel[...], 1, 0)
        value_ids = got[10:14] * 32.0 + got[14:18]
        reward_ids = got[18:22] * 32.0 + got[22:26]
        for k in range(steps):
            ids[k, 0:1, part] = got[0:1]
            ids[k, 1:3, part] = got[1 + k : 3 + k]
            ids[k, 3:4, part] = got[6 + k : 7 + k]
            ids[k, 4:5, part] = value_ids[k : k + 1]
            ids[k, 5:6, part] = reward_ids[k : k + 1]

    for n, (src, dst) in enumerate(copies):
        pltpu.make_async_copy(src, dst, w_sem.at[n]).wait()

    head_sum[...] = jnp.zeros_like(head_sum)
    loss_out[...] = jnp.zeros_like(loss_out)

    def spread_norms(k, tower, with_shift):
        count = 2 * NORMS if with_shift else NORMS
        row = lax.broadcasted_iota(jnp.int32, (MISC_ROWS, count * LANES), 0)
        at = lax.broadcasted_iota(jnp.int32, (MISC_ROWS, count * LANES), 1) // LANES
        gain_row = GAIN_ROW + tower * NORMS
        shift_row = SHIFT_ROW + tower * NORMS
        pick = jnp.where((at < NORMS) & (row == gain_row + at), 8.0, 0.0)
        pick = pick + jnp.where((at >= NORMS) & (row == shift_row + at - NORMS), 0.5, 0.0)
        gb[:, 0 : count * LANES] = contract(misc[k], pick.astype(BF16), 0, 0)

    def gain_of(n):
        return gb[:, n * LANES : (n + 1) * LANES]

    def shift_of(n):
        return gb[:, (NORMS + n) * LANES : (NORMS + n + 1) * LANES]

    def lookup(k, tower):
        lo = ACT_ROW if tower == 0 else 0
        return slice(lo, lo + 32)

    def tower_forward(k, tower):
        slot = lax.rem(k, 2)
        act = acts.at[slot, tower]
        spread_norms(k, tower, True)
        act[0] = current[...]
        look = lookup(k, tower)
        for part in chunks:
            first = contract(weights[k, 5 * tower], act[0, :, part], 0, 0)
            first = first + contract(misc[k, look], onehot[look, part], 0, 0)
            for n, sub in enumerate(subs(part)):
                out, slope, unit, inverse = norm_forward(
                    first[:, n * LANES : (n + 1) * LANES], gain_of(0), shift_of(0), None
                )
                resid[:, sub] = out
                act[1, :, sub] = out.astype(BF16)
                act[5, :, sub] = unit.astype(BF16)
                act[10, :, sub] = slope.astype(BF16)
                inv[2 * k + tower, 0:1, sub] = inverse
        for j in range(2):
            for part in chunks:
                pre = contract(weights[k, 5 * tower + 1 + 2 * j], act[1 + j, :, part], 0, 0)
                for n, sub in enumerate(subs(part)):
                    at = 1 + 2 * j
                    out, slope, unit, inverse = norm_forward(
                        pre[:, n * LANES : (n + 1) * LANES], gain_of(at), shift_of(at), None
                    )
                    act[3 + j, :, sub] = out.astype(BF16)
                    act[5 + at, :, sub] = unit.astype(BF16)
                    act[10 + at, :, sub] = slope.astype(BF16)
                    inv[2 * k + tower, at : at + 1, sub] = inverse
            for part in chunks:
                post = contract(weights[k, 5 * tower + 2 + 2 * j], act[3 + j, :, part], 0, 0)
                for n, sub in enumerate(subs(part)):
                    at = 2 + 2 * j
                    out, slope, unit, inverse = norm_forward(
                        post[:, n * LANES : (n + 1) * LANES], gain_of(at), shift_of(at), resid[:, sub]
                    )
                    if j == 0:
                        resid[:, sub] = out
                        act[2, :, sub] = out.astype(BF16)
                    else:
                        current[:, sub] = out.astype(BF16)
                    act[5 + at, :, sub] = unit.astype(BF16)
                    act[10 + at, :, sub] = slope.astype(BF16)
                    inv[2 * k + tower, at : at + 1, sub] = inverse

    def softmax_block(pieces, target, live):
        top = None
        for start, stop, low, high in pieces:
            part = logits[start:stop]
            if (low, high) != (start, stop):
                row = lax.broadcasted_iota(jnp.int32, part.shape, 0) + start
                part = jnp.where((row >= low) & (row < high), part, -jnp.inf)
            best = jnp.max(part, axis=0, keepdims=True)
            top = best if top is None else jnp.maximum(top, best)
        total = None
        hit = None
        for start, stop, low, high in pieces:
            part = logits[start:stop] - top
            row = lax.broadcasted_iota(jnp.int32, part.shape, 0) + start
            found = jnp.sum(jnp.where(row == target, part, 0.0), axis=0, keepdims=True)
            expo = jnp.exp(part)
            if (low, high) != (start, stop):
                keep = (row >= low) & (row < high)
                expo = jnp.where(keep, expo, 0.0)
                logits[start:stop] = jnp.where(keep, expo, logits[start:stop])
            else:
                logits[start:stop] = expo
            amount = jnp.sum(expo, axis=0, keepdims=True)
            total = amount if total is None else total + amount
            hit = found if hit is None else hit + found
        return live * (jnp.log(total) - hit), live / total

    def head_pass(k):
        slot = lax.rem(k, 2)
        for part in chunks:
            for sub in subs(part):
                live = jnp.where(ids[k, 0:1, sub] > k.astype(F32), 1.0, 0.0)
                value_at = ids[k, 4:5, sub].astype(jnp.int32)
                reward_at = ids[k, 5:6, sub].astype(jnp.int32) + bins
                policy_at = ids[k, 2:3, sub].astype(jnp.int32) + 2 * bins
                chance_at = ids[k, 3:4, sub].astype(jnp.int32)
                logits[...] = contract(head[...], current[:, sub], 0, 0)
                edge_a = bins // 8 * 8
                edge_b = 2 * bins // 8 * 8
                loss = None
                scales = []
                for pieces, target in (
                    (((0, edge_a, 0, edge_a), (edge_a, edge_a + 8, edge_a, bins)), value_at),
                    (
                        (
                            (edge_a, edge_a + 8, bins, edge_a + 8),
                            (edge_a + 8, edge_b, edge_a + 8, edge_b),
                            (edge_b, edge_b + 8, edge_b, 2 * bins),
                        ),
                        reward_at,
                    ),
                    (((edge_b, edge_b + 8, 2 * bins, head_width),), policy_at),
                ):
                    lost, scale = softmax_block(pieces, target, live)
                    loss = lost if loss is None else loss + lost
                    scales.append(scale)
                low_a = bins // 16 * 16
                low_b = 2 * bins // 16 * 16
                for start, stop in (
                    (0, low_a),
                    (low_a, low_a + 16),
                    (low_a + 16, low_b),
                    (low_b, low_b + 16),
                ):
                    row = lax.broadcasted_iota(jnp.int32, (stop - start, LANES), 0) + start
                    expo = logits[start:stop]
                    if stop <= bins:
                        delta = expo * scales[0] - jnp.where(row == value_at, live, 0.0)
                    elif start >= bins and stop <= 2 * bins:
                        delta = expo * scales[1] - jnp.where(row == reward_at, live, 0.0)
                    else:
                        scale = jnp.where(row < bins, scales[0], jnp.where(row < 2 * bins, scales[1], scales[2]))
                        delta = expo * scale
                        for target in (value_at, reward_at, policy_at):
                            delta = delta - jnp.where(row == target, live, 0.0)
                        delta = jnp.where(row < head_width, delta, 0.0)
                    dlogits[start:stop, sub] = delta.astype(BF16)
                if low_b + 16 < head_pad:
                    dlogits[low_b + 16 : head_pad, sub] = jnp.zeros((head_pad - low_b - 16, LANES), BF16)
                chance_logit = contract(chance_head[...], acts[slot, 1, 0, :, sub], 0, 0)
                chance_logit = chance_logit - jnp.max(chance_logit, axis=0, keepdims=True)
                expo = jnp.exp(chance_logit)
                total = jnp.sum(expo, axis=0, keepdims=True)
                row = lax.broadcasted_iota(jnp.int32, chance_logit.shape, 0)
                hot = row == chance_at
                hit = jnp.sum(jnp.where(hot, chance_logit, 0.0), axis=0, keepdims=True)
                loss = loss + live * (jnp.log(total) - hit)
                delta = expo * (live / total) - jnp.where(hot, live, 0.0)
                dchance[k, :, sub] = delta.astype(BF16)
                loss_out[0:1] += loss
        head_sum[:, 0:head_pad] += contract(current[...], dlogits[...], 1, 1)
        head_sum[:, head_pad : head_pad + 32] += contract(acts[slot, 1, 0], dchance[k], 1, 1)
        for part in chunks:
            head_back[k, :, part] = contract(head[...], dlogits[:, part], 1, 0)

    def make_onehot(k):
        row = lax.broadcasted_iota(jnp.int32, (MISC_ROWS, rows), 0)
        chance_at = ids[k, 3:4].astype(jnp.int32)
        action_at = ids[k, 1:2].astype(jnp.int32) + ACT_ROW
        onehot[...] = jnp.where((row == chance_at) | (row == action_at), 1.0, 0.0).astype(BF16)

    def spill_copy(k):
        return pltpu.make_async_copy(acts.at[lax.rem(k, 2)], spill.at[k], spill_sem.at[k])

    def fill_copy(k):
        return pltpu.make_async_copy(spill.at[k], acts.at[lax.rem(k, 2)], spill_sem.at[2 + k])

    @pl.loop(0, steps)
    def _(k):
        @pl.when(k >= 2)
        def _():
            spill_copy(k - 2).wait()

        make_onehot(k)
        tower_forward(k, 0)
        tower_forward(k, 1)
        head_pass(k)

        @pl.when(k < steps - 2)
        def _():
            spill_copy(k).start()

    def norm_backward(d_out, slope, unit, gain, inverse, at, first):
        d_two = d_out * slope.astype(F32)
        unit = unit.astype(F32)
        weighted = d_two * unit
        if first:
            acc_dy[at] = d_two
            acc_p[at] = weighted
        else:
            acc_dy[at] += d_two
            acc_p[at] += weighted
        d_unit = d_two * gain
        mean = jnp.sum(d_unit, axis=0, keepdims=True) * (1.0 / WIDE)
        along = jnp.sum(weighted * gain, axis=0, keepdims=True)
        return ((d_unit - mean - unit * along) * inverse).astype(BF16), d_two

    def tower_backward(k, tower, last):
        slot = lax.rem(k, 2)
        act = acts.at[slot, tower]
        spread_norms(k, tower, False)

        def norm_of(d_out, at, sub):
            return norm_backward(
                d_out,
                act[10 + at, :, sub],
                act[5 + at, :, sub],
                gain_of(at),
                inv[2 * k + tower, at : at + 1, sub],
                at,
                sub.start == 0,
            )

        for j in (1, 0):
            outer = 2 + 2 * j
            inner = 1 + 2 * j
            for part in chunks:
                for sub in subs(part):
                    d_post, d_two = norm_of(grad[:, sub], outer, sub)
                    prod_a[:, sub] = d_post
                    grad[:, sub] = 0.5 * d_two
            for part in chunks:
                d_mid = contract(weights[k, 5 * tower + 2 + 2 * j], prod_a[:, part], 1, 0)
                for n, sub in enumerate(subs(part)):
                    d_pre, _ = norm_of(d_mid[:, n * LANES : (n + 1) * LANES], inner, sub)
                    prod_b[:, sub] = d_pre
            tower_out[k, 5 * tower + 2 + 2 * j] = contract(act[3 + j], prod_a[...], 1, 1)
            for part in chunks:
                grad[:, part] += contract(weights[k, 5 * tower + 1 + 2 * j], prod_b[:, part], 1, 0)
            tower_out[k, 5 * tower + 1 + 2 * j] = contract(act[1 + j], prod_b[...], 1, 1)
        for part in chunks:
            for sub in subs(part):
                d_first, _ = norm_of(grad[:, sub], 0, sub)
                prod_a[:, sub] = d_first
        look = lookup(k, tower)
        tower_out[k, 5 * tower] = contract(act[0], prod_a[...], 1, 1)
        got = contract(onehot[look], prod_a[...], 1, 1)
        if tower == 0:
            misc_grad[k, ACT_ROW : ACT_ROW + action_count] = got[0:action_count]
        else:
            misc_grad[k, 0:32] = got
        ones = jnp.ones((16, LANES), BF16)
        for n in range(NORMS):
            total = contract(ones, acc_p[n].astype(BF16), 1, 1)
            misc_grad[k, GAIN_ROW + NORMS * tower + n : GAIN_ROW + NORMS * tower + n + 1] = 8.0 * total[0:1]
            total = contract(ones, acc_dy[n].astype(BF16), 1, 1)
            misc_grad[k, SHIFT_ROW + NORMS * tower + n : SHIFT_ROW + NORMS * tower + n + 1] = 0.5 * total[0:1]

    @pl.loop(0, steps)
    def _(back):
        k = steps - 1 - back

        @pl.when(k < steps - 2)
        def _():
            fill_copy(k).wait()

        make_onehot(k)

        @pl.when(back == 0)
        def _():
            grad[...] = head_back[k]

        @pl.when(back > 0)
        def _():
            grad[...] = (0.5 * grad[...]).astype(BF16).astype(F32) + head_back[k]

        tower_backward(k, 1, False)
        for part in chunks:
            grad[:, part] = contract(weights[k, 5], prod_a[:, part], 1, 0) + contract(
                chance_head[...], dchance[k, :, part], 1, 0
            )
        tower_backward(k, 0, True)

        @pl.when(k > 0)
        def _():
            for part in chunks:
                grad[:, part] = contract(weights[k, 0], prod_a[:, part], 1, 0)

        @pl.when(k == 0)
        def _():
            for part in chunks:
                latent_out[part] = 0.5 * contract(prod_a[:, part], weights[0, 0], 0, 1)

        @pl.when(k >= 2)
        def _():
            fill_copy(k - 2).start()

    misc_out[...] = misc_grad[...]
    head_out[...] = head_sum[...]


def per_device(
    latent, lengths, actions, chances, value_bins, reward_bins,
    entry_w, action_w, chance_w, block_w, gain_w, shift_w, state_head, chance_head,
):
    full = tuple(
        lax.all_gather(source, "section", axis=0, tiled=True)
        for source in (entry_w, block_w, action_w, chance_w, gain_w, shift_w)
    )
    steps = full[0].shape[0]
    rows = latent.shape[0] // steps
    feat = latent.shape[1]
    head_width = state_head.shape[1]
    head_pad = -(-head_width // LANES) * LANES
    gains = full[4].reshape(steps, -1, feat)
    shifts = full[5].reshape(steps, -1, feat)
    vmem = pl.BlockSpec(memory_space=pltpu.VMEM)
    anys = pl.BlockSpec(memory_space=pl.ANY)
    scratch = [
        pltpu.VMEM((steps, 10, feat, feat), BF16),
        pltpu.VMEM((steps, MISC_ROWS, feat), BF16),
        pltpu.VMEM((feat, head_pad), BF16),
        pltpu.VMEM((2, 2, 15, feat, rows), BF16),
        pltpu.VMEM((2 * steps, 8, rows), F32),
        pltpu.VMEM((steps, 8, rows), F32),
        pltpu.VMEM((MISC_ROWS, rows), BF16),
        pltpu.VMEM((feat, rows), BF16),
        pltpu.VMEM((feat, rows), F32),
        pltpu.VMEM((feat, rows), BF16),
        pltpu.VMEM((feat, rows), BF16),
        pltpu.VMEM((feat, rows), F32),
        pltpu.VMEM((feat, 2 * NORMS * LANES), F32),
        pltpu.VMEM((NORMS, feat, LANES), F32),
        pltpu.VMEM((NORMS, feat, LANES), F32),
        pltpu.VMEM((head_pad, LANES), F32),
        pltpu.VMEM((head_pad, rows), BF16),
        pltpu.VMEM((steps, 32, rows), BF16),
        pltpu.VMEM((steps, feat, rows), F32),
        pltpu.VMEM((feat, head_pad + LANES), F32),
        pltpu.VMEM((steps, MISC_ROWS, feat), F32),
        pltpu.VMEM((steps * WIDE, WIDE), BF16),
        pltpu.VMEM((32, latent.shape[0]), F32),
        pltpu.SemaphoreType.DMA((steps * 10,)),
        pltpu.SemaphoreType.DMA((4,)),
    ]
    outs = pl.pallas_call(
        kernel,
        out_shape=(
            jax.ShapeDtypeStruct((rows, feat), F32),
            jax.ShapeDtypeStruct((steps, 10, feat, feat), F32),
            jax.ShapeDtypeStruct((steps, MISC_ROWS, feat), F32),
            jax.ShapeDtypeStruct((feat, head_pad + LANES), F32),
            jax.ShapeDtypeStruct((8, LANES), F32),
            jax.ShapeDtypeStruct((steps - 2, 2, 15, feat, rows), BF16),
        ),
        in_specs=[vmem] * 6 + [anys] * 2 + [vmem] * 6,
        out_specs=(vmem,) * 5 + (anys,),
        scratch_shapes=scratch,
        compiler_params=pltpu.CompilerParams(vmem_limit_bytes=62 * 2**20),
    )(
        latent, lengths.reshape(1, -1), actions, chances, value_bins, reward_bins,
        full[0], full[1], full[2], full[3], gains, shifts, state_head, chance_head,
    )
    latent_grad, tower_grad, misc_grad, head_grad, loss, _ = outs
    tower_grad = lax.psum_scatter(tower_grad.astype(BF16), "section", scatter_dimension=0, tiled=True).astype(F32)
    misc_grad = lax.psum_scatter(misc_grad, "section", scatter_dimension=0, tiled=True)
    tower_grad, misc_grad = lax.psum((tower_grad, misc_grad), "dp")
    head_grad, loss = lax.psum((head_grad, jnp.sum(loss)), ("section", "dp"))
    scale = 1.0 / (latent.shape[0] * lax.axis_size("dp"))
    tower_grad = (tower_grad * scale)[0].reshape(2, 5, feat, feat)
    misc_grad = (misc_grad * scale)[0]
    act_n = action_w.shape[1]
    return (
        latent_grad.reshape(rows, 1, feat),
        tower_grad[:, 0][None],
        misc_grad[None, ACT_ROW : ACT_ROW + act_n],
        misc_grad[None, 0:32],
        tower_grad[:, 1:].reshape(1, 2, 2, 2, feat, feat),
        misc_grad[GAIN_ROW : GAIN_ROW + 10].reshape(1, 2, 5, feat),
        misc_grad[SHIFT_ROW : SHIFT_ROW + 10].reshape(1, 2, 5, feat),
        head_grad[:, :head_width] * scale,
        head_grad[:, head_pad : head_pad + 32] * scale,
        loss * scale,
    )


def solution(mesh):
    placed = (
        P("dp", None), P("dp"), P(None, "dp"), P(None, "dp"), P(None, "dp"), P(None, "dp"),
        P("section", None, None, None), P("section", None, None), P("section", None, None),
        P("section", None, None, None, None, None), P("section", None, None, None), P("section", None, None, None),
        P(), P(),
    )
    return jax.shard_map(
        per_device,
        mesh=mesh,
        in_specs=placed,
        out_specs=(
            P("dp", "section", None), P("section", None, None, None), P("section", None, None),
            P("section", None, None), P("section", None, None, None, None, None),
            P("section", None, None, None), P("section", None, None, None), P(), P(), P(),
        ),
        check_vma=False,
    )
```

time: 1340 us -> 554 us (0.41); the launches traced: 1320 us -> 553 us
  matrix products: 423 us -> 0 us
  other arithmetic: 255 us -> 11.1 us
  local copies, waits for them, and re-layouts: 233 us -> 14.1 us
  Pallas kernels: 0 us -> 103 us
  waiting for transfers between devices: 188 us -> 270 us
  loops' own time: 42.4 us -> 0 us
  blocking collectives: 157 us -> 139 us
    dot_general x320 -> x0, matrix products: 423 us -> none  [the longest x96 185 us: product_nt(): lax.dot_general(left_mat, right_mat, (((1,), (1,)), ((), ())), preferred_...]
    pallas_call x0 -> x1, Pallas kernels: none -> 103 us  [per_device(): pl.pallas_call(kernel, out_shape=(jax.ShapeDtypeStruct((rows, feat), F32)...]
    reduce_sum x188 -> x1, other arithmetic: 101 us -> 0.6 us  [per_device(): head_grad, loss = lax.psum((head_grad, jnp.sum(loss)), ('section', 'dp'))]
    concatenate x8 -> x0, local copies, waits for them, and re-layouts: 56.7 us -> none  [step_forward(): jnp.concatenate([grad_value, grad_reward, grad_policy], axis=1)]
    while x2098 -> x0, local copies, waits for them, and re-layouts: 55.9 us -> none
    another operation x76 -> x0, other arithmetic: 55.1 us -> none
    slice x44 -> x4, local copies, waits for them, and re-layouts: 57.5 us -> 2.74 us  [the longest x1 1.53 us: per_device(): tower_grad[:, 1:].reshape(1, 2, 2, 2, feat, feat)]
    psum x1 -> x2, waiting for transfers between devices: 86.8 us -> 139 us  [the longest x1 133 us: per_device(): head_grad, loss = lax.psum((head_grad, jnp.sum(loss)), ('section', 'dp'))]
  transfers between devices with their start and end apart: 6 -> 6, of which waited for: 4 -> 5; matrix products, arithmetic and copies ran while one was open for 4% -> 4% of each run, Pallas kernels for 0% -> 0%
where the time goes in v1:
time: 554 us; the launch traced here: 553 us
  waiting for transfers between devices  270 us (49%)
  blocking collectives  139 us (25%)
  Pallas kernels  103 us (19%)
  between operations  16 us (3%)
  local copies, waits for them, and re-layouts  14.1 us (3%)
  other arithmetic  11.1 us (2%)
    psum x1, waiting for transfers between devices, per_device(): head_grad, loss = lax.psum((head_grad, jnp.sum(loss)), ('section', 'dp'))  133 us
    pallas_call x1, Pallas kernels, per_device(): pl.pallas_call(kernel, out_shape=(jax.ShapeDtypeStruct((rows, feat), F32)...  103 us
    unnamed x8, waiting for transfers between devices  84.9 us
    psum x1, blocking collectives, per_device(): tower_grad, misc_grad = lax.psum((tower_grad, misc_grad), 'dp')  65.6 us
    all_gather x2, waiting for transfers between devices, per_device(): lax.all_gather(source, 'section', axis=0, tiled=True)  46.1 us
    psum x1, blocking collectives, per_device(): head_grad, loss = lax.psum((head_grad, jnp.sum(loss)), ('section', 'dp'))  39.6 us
    all_gather x4, blocking collectives, per_device(): lax.all_gather(source, 'section', axis=0, tiled=True)  34.3 us
  transfers between devices with their start and end apart: 6, of which 5 were waited for; matrix products, arithmetic and copies ran while one was open for 4% of the time, Pallas kernels for 0%

profile of v1, /device:TPU:0, one launch (start us, length us, event | category | flops | bytes accessed | tf_op | source)
XLA Modules:
  0.0 553.2 jit_solution(11851538713518016680)
XLA Ops:
  7.2 0.7 all-gather.3.cloned.1.call-update
  8.0 0.7 all-gather.5.cloned.1.call-update
  8.7 9.7 %all_gather.22 = bf16[4,2,5,256]{3,1,2,0:T(2,128)(2,1)S(1)} all-gather(bf16[1,2,5,256]{3,1,2,0:T(2,128)(2,1)} %param.24), channel_id=1, replica_groups=mesh['section'=4,'dp'=8] {'section'}, dimensions={0}, use_global_device_ids=true | all-gather | bytes 25600 | tf_op jit(solution)/shard_map/all_gather | solution.py:428
  18.5 0.6 copy.48.gains
  19.1 8.0 %all_gather.23 = bf16[4,2,5,256]{3,1,2,0:T(2,128)(2,1)S(1)} all-gather(bf16[1,2,5,256]{3,1,2,0:T(2,128)(2,1)} %param.25), channel_id=1, replica_groups=mesh['section'=4,'dp'=8] {'section'}, dimensions={0}, use_global_device_ids=true | all-gather | bytes 25600 | tf_op jit(solution)/shard_map/all_gather | solution.py:428
  27.1 0.6 copy.49.shifts
  27.8 1.4 copy.51.chance_head
  29.2 2.1 copy.50.state_head
  31.4 7.8 %all_gather.20.action_w = bf16[4,4,256]{2,1,0:T(4,128)(2,1)} all-gather(bf16[1,4,256]{2,1,0:T(4,128)(2,1)S(1)} %copy-done.3), channel_id=1, replica_groups=mesh['section'=4,'dp'=8] {'section'}, dimensions={0}, use_global_device_ids=true | all-gather | bytes 10240 | tf_op jit(solution)/shard_map/all_gather | solution.py:428
  39.2 8.7 %all_gather.21.chance_w = bf16[4,32,256]{2,1,0:T(8,128)(2,1)} all-gather(bf16[1,32,256]{2,1,0:T(8,128)(2,1)S(1)} %copy-done.1), channel_id=1, replica_groups=mesh['section'=4,'dp'=8] {'section'}, dimensions={0}, use_global_device_ids=true | all-gather | bytes 81920 | tf_op jit(solution)/shard_map/all_gather | solution.py:428
  47.9 46.1 %all-gather.5.cloned.1.call-done.blocks = bf16[4,2,2,2,256,256]{5,4,3,2,1,0:T(8,128)(2,1)} async-done(((bf16[1,2,2,2,256,256]{5,4,3,2,1,0:T(8,128)(2,1)}), bf16[4,2,2,2,256,256]{5,4,3,2,1,0:T(8,128)(2,1)}) %all-gather.5.cloned.1.call-update) | async-done | bytes 4194320 | tf_op jit(solution)/shard_map/all_gather | solution.py:428
  94.0 102.9 %shard_map.213 = (f32[768,256]{1,0:T(8,128)}, f32[4,10,256,256]{3,2,1,0:T(8,128)}, f32[4,64,256]{2,1,0:T(8,128)}, f32[256,1408]{1,0:T(8,128)}, f32[8,128]{1,0:T(8,128)}, /*index=5*/bf16[2,2,15,256,768]{4,3,2,1,0:T(8,128)(2,1)}) custom-call(bf16[3072,256]{1,0:T(8,128)(2,1)} %latent.1, s32[1,3072]{1,0:T(1,128)} %bitcast.17, s32[5,3072]{1,0:T(8,128)} %actions.1, ...), custom_call_target="tpu_custom_call" | custom-call | tf_op jit(solution)/shard_map/pallas_call | solution.py:467
  196.9 24.2 %reduce-scatter.9.cloned.1.call-done = f32[1,64,256]{2,1,0:T(8,128)} async-done(((f32[4,64,256]{2,1,0:T(8,128)}), f32[1,64,256]{2,1,0:T(8,128)}) %reduce-scatter.9.cloned.1.call-update) | async-done | bytes 65552
  221.8 7.0 %convert_element_type.6 = bf16[4,10,256,256]{3,2,1,0:T(8,128)(2,1)} convert(f32[4,10,256,256]{3,2,1,0:T(8,128)} %get-tuple-element.16) | non-fusion elementwise | flops 2621440 | bytes 15728640 | tf_op jit(solution)/shard_map/convert_element_type | solution.py:486
  228.8 0.7 copy-done.2
  229.5 0.6 reduce_sum.9
  230.1 39.6 %psum.31 = f32[]{:T(128)} all-reduce(f32[]{:T(128)} %reduce_sum.9), channel_id=1, replica_groups=mesh['section'=4,'dp'=8] {'section','dp'}, use_global_device_ids=true, to_apply=%region_6.0 | all-reduce | flops 1 | bytes 8 | tf_op jit(solution)/shard_map/psum | solution.py:489
  269.6 1.7 copy.53
  271.9 5.1 all-reduce.6.cloned.1.call-done
  277.1 0.8 broadcast_multiply_fusion.1
  278.5 0.6 slice.38
  279.1 0.6 copy.55
  279.8 0.6 copy.54
  280.4 133.4 %all-reduce.8.cloned.1.call-done = f32[256,1408]{1,0:T(8,128)} async-done(((f32[256,1408]{1,0:T(8,128)}), f32[256,1408]{1,0:T(8,128)}) %all-reduce.8.cloned.1.call-update) | async-done | bytes 1441808 | tf_op jit(solution)/shard_map/psum | solution.py:489
  413.8 0.9 slice_multiply_fusion.1
  414.7 0.7 copy.57
  415.4 1.4 slice_multiply_fusion
  416.8 1.4 copy.56
  418.2 58.8 %reduce-scatter.7.cloned.1.call-done = bf16[1,10,256,256]{3,2,1,0:T(8,128)(2,1)} async-done(((bf16[4,10,256,256]{3,2,1,0:T(8,128)(2,1)}), bf16[1,10,256,256]{3,2,1,0:T(8,128)(2,1)}) %reduce-scatter.7.cloned.1.call-update) | async-done | bytes 1310736
  477.0 65.6 %all-reduce.9 = f32[1,10,256,256]{3,2,1,0:T(8,128)S(1)} all-reduce(bf16[1,10,256,256]{3,2,1,0:T(8,128)(2,1)} %reduce-scatter.7.cloned.1.call-done), channel_id=1, replica_groups=mesh['section'=4,'dp'=8] {'dp'}, use_global_device_ids=true, to_apply=%region_1.0 | all-reduce | flops 655360 | bytes 3932160 | tf_op jit(solution)/shard_map/psum | solution.py:488
  542.9 0.8 slice_bitcast_fusion
  543.7 1.5 slice.39
  (25 shorter events, 1.8 us)
Async XLA Ops:
  7.2 24.2 %copy-start.3 = (bf16[1,4,256]{2,1,0:T(4,128)(2,1)S(1)}, bf16[1,4,256]{2,1,0:T(4,128)(2,1)}, u32[]{:S(2)}) copy-start(bf16[1,4,256]{2,1,0:T(4,128)(2,1)} %param.21) | copy-start | bytes 6148
  7.2 32.0 %copy-start.1 = (bf16[1,32,256]{2,1,0:T(8,128)(2,1)S(1)}, bf16[1,32,256]{2,1,0:T(8,128)(2,1)}, u32[]{:S(2)}) copy-start(bf16[1,32,256]{2,1,0:T(8,128)(2,1)} %param.22) | copy-start | bytes 49156
  7.2 40.7 %all-gather.3.cloned.1.call-start = ((), (), s32[]{:S(2)}) async-start(), calls=%async_computation.2 | async-start | bytes 1310720 | tf_op jit(solution)/shard_map/all_gather | solution.py:428
  7.9 86.1 %all-gather.5.cloned.1.call-start = ((), (), s32[]{:S(2)}) async-start(), calls=%async_computation.3 | async-start | bytes 5242880 | tf_op jit(solution)/shard_map/all_gather | solution.py:428
  8.7 212.4 %reduce-scatter.9.cloned.1.call-start = ((), (), s32[]{:S(2)}) async-start(), calls=%async_computation.7 | async-start | bytes 327680
  196.9 80.2 %all-reduce.6.cloned.1.call-start = ((), (), s32[]{:S(2)}) async-start(), calls=%async_computation.4 | async-start | bytes 131072 | tf_op jit(solution)/shard_map/psum | solution.py:488
  221.1 192.6 %all-reduce.8.cloned.1.call-start = ((), (), s32[]{:S(2)}) async-start(), calls=%async_computation.5 | async-start | bytes 2883584 | tf_op jit(solution)/shard_map/psum | solution.py:489
  221.7 255.3 %reduce-scatter.7.cloned.1.call-start = ((), (), s32[]{:S(2)}) async-start(), calls=%async_computation.6 | async-start | bytes 6553600
  228.8 0.7 copy-start.2
  228.8 40.8 %copy-start = (f32[768,256]{1,0:T(8,128)S(1)}, f32[768,256]{1,0:T(8,128)}, u32[]{:S(2)}) copy-start(f32[768,256]{1,0:T(8,128)} %get-tuple-element.15) | copy-start | bytes 2359300
Sparse Core Ops, SparseCore 0:
  9.9 29.5 all-gather.2
  41.3 52.6 all-gather.4
  197.0 24.0 reduce-scatter.8
  223.4 53.6 all-reduce.5
  282.8 130.9 all-reduce.7
  416.6 60.3 reduce-scatter.6

commit v2 on v1

--- a/solution.py
+++ b/solution.py
@@ -1,3 +1,5 @@
+import functools
+
 import jax
 import jax.numpy as jnp
 from jax import lax
@@ -46,56 +48,201 @@
     return out, slope, unit, inverse
 
 
+QUARTER = 320
+LAST = 384
+CHAIN = ((0, 1), (1, 2), (2, 3), (3, 4), (4, 6), (6, 8), (8, 10))
+EARLY = (7, 0, 1, 2, 3, 4)
+LATE = (5, 6)
+MESH = pl.DeviceIdType.MESH
+
+
+def when(condition, action):
+    if isinstance(condition, bool):
+        if condition:
+            action()
+    else:
+        pl.when(condition)(action)
+
+
 def kernel(
+    scale, near_count, far_count,
     latent, lengths, actions, chances, values, rewards, entry, blocks, action_w, chance_w, gains, shifts,
     state_head, chance_head,
-    latent_out, tower_out, misc_out, head_out, loss_out, spill,
+    latent_out, entry_out, block_out, action_out, chance_out, gain_out, shift_out, head_out, chead_out, loss_out, spill,
     weights, misc, head, acts, inv, ids, onehot, current, resid, prod_a, prod_b, grad, gb, acc_dy, acc_p,
-    logits, dlogits, dchance, head_back, head_sum, misc_grad, sel, stage,
-    w_sem, spill_sem,
+    logits, dlogits, dchance, head_back, head_sum, chead_sum, misc_grad, loss_sum, sel, stage, states,
+    sent, core_in, core_sum, part_in, part_sum, near_in, far_in, quarter, whole, other, misc_in, loss_in,
+    load_sem, spill_sem, chain_send, chain_recv, give_send, step_recv, pass_send, pair_send, pair_recv,
+    core_send, core_recv, part_send, part_recv, near_send, near_recv, far_send, far_recv,
+    fill_send, fill_recv, own_send, own_recv, lane_send, lane_recv, extra_send, extra_recv, loss_send, loss_recv,
 ):
     section = lax.axis_index("section")
+    line = lax.axis_index("dp")
+    core = lax.rem(line, 2)
+    near = lax.rem(line // 2, near_count)
+    far = line // 2 // near_count
+    mate = line + 1 - 2 * core
     rows = current.shape[1]
     steps = weights.shape[0]
     feat = WIDE
-    head_width = state_head.shape[1]
+    head_width = state_head.shape[0]
     bins = (head_width - action_w.shape[1]) // 2
-    head_pad = head.shape[1]
+    head_pad = head.shape[0]
     action_count = action_w.shape[1]
+    chance_count = chance_w.shape[1]
     chunks = [slice(c, c + WIDE) for c in range(0, rows, WIDE)]
+    batches = 2 * steps
 
     def subs(part):
         return [slice(c, c + LANES) for c in range(part.start, part.stop, LANES)]
 
-    copies = []
-    for k in range(steps):
-        for t in range(2):
-            copies.append((entry.at[k, t], weights.at[k, 5 * t]))
-            for j in range(2):
-                for i in range(2):
-                    copies.append((blocks.at[k, t, j, i], weights.at[k, 5 * t + 1 + 2 * j + i]))
-    for n, (src, dst) in enumerate(copies):
-        pltpu.make_async_copy(src, dst, w_sem.at[n]).start()
-
-    for k in range(steps):
-        packed = jnp.concatenate(
-            [
-                chance_w[k].astype(F32),
-                action_w[k].astype(F32),
-                gains[k].astype(F32),
-                shifts[k].astype(F32),
-                jnp.zeros((MISC_ROWS - SHIFT_ROW - 2 * NORMS, feat), F32),
-            ],
-            axis=0,
+    def near_line(offset):
+        return (far * near_count + lax.rem(near + offset, near_count)) * 2 + core
+
+    def far_line(offset):
+        return (lax.rem(far + offset, far_count) * near_count + near) * 2 + core
+
+    def section_at(offset):
+        return lax.rem(section + offset, steps)
+
+    barrier = pltpu.get_barrier_semaphore()
+    peers = [{"dp": mate}]
+    peers += [{"section": section_at(o)} for o in range(1, steps)]
+    peers += [{"dp": near_line(o)} for o in range(1, near_count)]
+    peers += [{"dp": far_line(o)} for o in range(1, far_count)]
+    for peer in peers:
+        pl.semaphore_signal(barrier, inc=1, device_id=peer, device_id_type=MESH)
+
+    loads = [(entry.at[0, 0], weights.at[section, 0]), (blocks.at[0, 0], weights.at[section, 1:5])]
+    loads += [(entry.at[0, 1], weights.at[section, 5]), (blocks.at[0, 1], weights.at[section, 6:10])]
+    loads += [(latent, states)]
+    loads = [pltpu.make_async_copy(src, dst, load_sem.at[n]) for n, (src, dst) in enumerate(loads)]
+    for load in loads:
+        load.start()
+    head[head_width // 16 * 16 : head_pad] = jnp.zeros((head_pad - head_width // 16 * 16, feat), BF16)
+    head[0:head_width] = state_head[...]
+
+    packed = jnp.concatenate(
+        [
+            chance_w[0].astype(F32),
+            action_w[0].astype(F32),
+            gains[0, 0].astype(F32),
+            gains[0, 1].astype(F32),
+            shifts[0, 0].astype(F32),
+            shifts[0, 1].astype(F32),
+            jnp.zeros((MISC_ROWS - SHIFT_ROW - 2 * NORMS, feat), F32),
+        ],
+        axis=0,
+    )
+    misc[section] = packed.astype(BF16)
+
+    def send(src, dst, sender, receiver, peer):
+        return pltpu.make_async_remote_copy(
+            src_ref=src, dst_ref=dst, send_sem=sender, recv_sem=receiver, device_id=peer, device_id_type=MESH
         )
-        misc[k] = packed.astype(BF16)
-    head[...] = jnp.zeros_like(head)
-    head[:, 0:head_width] = state_head[...]
-
-    steps_of = steps
-    pick_at = lax.broadcasted_iota(jnp.int32, (steps_of * WIDE, WIDE), 0)
-    pick_to = lax.broadcasted_iota(jnp.int32, (steps_of * WIDE, WIDE), 1)
-    sel[...] = (pick_at == steps_of * pick_to + section).astype(F32).astype(BF16)
+
+    def landed(dst, receiver):
+        send(dst, dst, load_sem.at[7], receiver, {"dp": mate}).wait_recv()
+
+    place = jnp.where(section >= 2, 5 - section, section)
+    after = lax.rem(place + 1 + 2 * core, steps)
+    after = jnp.where(after >= 2, 5 - after, after)
+    hops = jnp.where(core == 0, place, lax.rem(steps - place, steps))
+    side_a = section + 1 - 2 * lax.rem(section, 2)
+    side_b = lax.rem(section + 2, steps)
+    pass_step = jnp.where(core == 0, side_a, side_b)
+    pass_to = jnp.where(core == 0, side_b, side_a)
+
+    def half_of(step, first, last, part):
+        at = pl.multiple_of(part * (feat // 2), feat // 2)
+        return weights.at[step, first:last, pl.ds(at, feat // 2)]
+
+    def misc_half(step, part):
+        return misc.at[step, pl.ds(pl.multiple_of(part * (MISC_ROWS // 2), MISC_ROWS // 2), MISC_ROWS // 2)]
+
+    def piece(step, n, part):
+        if isinstance(step, int) and step == 0:
+            return misc_half(0, part) if n == 7 else half_of(0, *CHAIN[n], part)
+        return misc_half(step, part) if n == 2 else half_of(step, 5 * n, 5 * n + 5, part)
+
+    def chain(n):
+        ref = piece(0, n, core)
+        return send(ref, ref, chain_send.at[n], chain_recv.at[n], {"section": after})
+
+    def give(way, n):
+        ref = piece(section, n, core)
+        return send(ref, ref, give_send.at[way, n], step_recv.at[section, n], {"section": (side_a, side_b)[way]})
+
+    def hand_on(n):
+        ref = piece(pass_step, n, core)
+        return send(ref, ref, pass_send.at[n], step_recv.at[pass_step, n], {"section": pass_to})
+
+    def pair(step, n):
+        ref = piece(step, n, core)
+        return send(ref, ref, pair_send.at[step, n], pair_recv.at[step, n], {"dp": mate})
+
+    def chain_on(order, onward):
+        def run():
+            for n in order:
+                landed(piece(0, n, core), chain_recv.at[n])
+                if onward:
+                    chain(n).start()
+                pair(0, n).start()
+
+        return run
+
+    def need_first(order):
+        def run():
+            for n in order:
+                landed(piece(0, n, 1 - core), pair_recv.at[0, n])
+
+        when(section != 0, run)
+
+    def hand_on_now(condition, pieces):
+        def run():
+            for n in pieces:
+                landed(piece(pass_step, n, core), step_recv.at[pass_step, n])
+                hand_on(n).start()
+
+        when(condition, run)
+
+    def pair_now(step, pieces):
+        def run():
+            for n in pieces:
+                pl.when(pass_step != step)(functools.partial(landed, piece(step, n, core), step_recv.at[step, n]))
+                pair(step, n).start()
+
+        when(section != step, run)
+
+    def need(step, pieces):
+        def run():
+            for n in pieces:
+                landed(piece(step, n, 1 - core), pair_recv.at[step, n])
+
+        when(section != step, run)
+
+    def give_now(way):
+        def run():
+            for n in (2, 0, 1):
+                give(way, n).start()
+
+        return run
+
+    pl.semaphore_wait(barrier, len(peers))
+    for load in loads[0:4]:
+        load.wait()
+
+    @pl.when(hops == 0)
+    def _():
+        for n in EARLY + LATE:
+            chain(n).start()
+
+    pl.when(section == 1)(give_now(0))
+    pl.when(section == 2)(give_now(1))
+
+    pick_at = lax.broadcasted_iota(jnp.int32, (steps * WIDE, WIDE), 0)
+    pick_to = lax.broadcasted_iota(jnp.int32, (steps * WIDE, WIDE), 1)
+    sel[...] = (pick_at == steps * pick_to + section).astype(F32).astype(BF16)
     stage[...] = jnp.zeros_like(stage)
     stage[0:1] = lengths[...].astype(F32)
     stage[1:6] = actions[...].astype(F32)
@@ -104,9 +251,11 @@
     stage[14:18] = (values[...] & 31).astype(F32)
     stage[18:22] = lax.shift_right_logical(rewards[...], 5).astype(F32)
     stage[22:26] = (rewards[...] & 31).astype(F32)
+    for load in loads[4:]:
+        load.wait()
     for n, part in enumerate(chunks):
-        rows_in = slice(n * steps_of * WIDE, (n + 1) * steps_of * WIDE)
-        current[:, part] = contract(latent[rows_in], sel[...], 0, 0).astype(BF16)
+        rows_in = slice(n * steps * WIDE, (n + 1) * steps * WIDE)
+        current[:, part] = contract(states[rows_in], sel[...], 0, 0).astype(BF16)
         got = contract(stage[:, rows_in].astype(BF16), sel[...], 1, 0)
         value_ids = got[10:14] * 32.0 + got[14:18]
         reward_ids = got[18:22] * 32.0 + got[22:26]
@@ -116,12 +265,17 @@
             ids[k, 3:4, part] = got[6 + k : 7 + k]
             ids[k, 4:5, part] = value_ids[k : k + 1]
             ids[k, 5:6, part] = reward_ids[k : k + 1]
-
-    for n, (src, dst) in enumerate(copies):
-        pltpu.make_async_copy(src, dst, w_sem.at[n]).wait()
-
     head_sum[...] = jnp.zeros_like(head_sum)
-    loss_out[...] = jnp.zeros_like(loss_out)
+    chead_sum[...] = jnp.zeros_like(chead_sum)
+    loss_sum[...] = jnp.zeros_like(loss_sum)
+
+    pl.when((hops == 1) | (hops == 2))(chain_on(EARLY + LATE, True))
+    pl.when(section == 1)(give_now(1))
+    pl.when(section == 2)(give_now(0))
+    pl.when(section == 3)(give_now(0))
+    pl.when(section == 3)(give_now(1))
+    pl.when(hops == 3)(chain_on(EARLY, False))
+    need_first(EARLY)
 
     def spread_norms(k, tower, with_shift):
         count = 2 * NORMS if with_shift else NORMS
@@ -216,16 +370,18 @@
             hit = found if hit is None else hit + found
         return live * (jnp.log(total) - hit), live / total
 
-    def head_pass(k):
+    def head_pass(k, tick):
         slot = lax.rem(k, 2)
         for part in chunks:
+            if part.start == WIDE:
+                tick()
             for sub in subs(part):
                 live = jnp.where(ids[k, 0:1, sub] > k.astype(F32), 1.0, 0.0)
                 value_at = ids[k, 4:5, sub].astype(jnp.int32)
                 reward_at = ids[k, 5:6, sub].astype(jnp.int32) + bins
                 policy_at = ids[k, 2:3, sub].astype(jnp.int32) + 2 * bins
                 chance_at = ids[k, 3:4, sub].astype(jnp.int32)
-                logits[...] = contract(head[...], current[:, sub], 0, 0)
+                logits[...] = contract(head[...], current[:, sub], 1, 0)
                 edge_a = bins // 8 * 8
                 edge_b = 2 * bins // 8 * 8
                 loss = None
@@ -268,7 +424,7 @@
                     dlogits[start:stop, sub] = delta.astype(BF16)
                 if low_b + 16 < head_pad:
                     dlogits[low_b + 16 : head_pad, sub] = jnp.zeros((head_pad - low_b - 16, LANES), BF16)
-                chance_logit = contract(chance_head[...], acts[slot, 1, 0, :, sub], 0, 0)
+                chance_logit = contract(chance_head[...], acts[slot, 1, 0, :, sub], 1, 0)
                 chance_logit = chance_logit - jnp.max(chance_logit, axis=0, keepdims=True)
                 expo = jnp.exp(chance_logit)
                 total = jnp.sum(expo, axis=0, keepdims=True)
@@ -278,11 +434,11 @@
                 loss = loss + live * (jnp.log(total) - hit)
                 delta = expo * (live / total) - jnp.where(hot, live, 0.0)
                 dchance[k, :, sub] = delta.astype(BF16)
-                loss_out[0:1] += loss
-        head_sum[:, 0:head_pad] += contract(current[...], dlogits[...], 1, 1)
-        head_sum[:, head_pad : head_pad + 32] += contract(acts[slot, 1, 0], dchance[k], 1, 1)
+                loss_sum[0:1] += loss
+        head_sum[...] += contract(dlogits[...], current[...], 1, 1)
+        chead_sum[...] += contract(dchance[k], acts[slot, 1, 0], 1, 1)
         for part in chunks:
-            head_back[k, :, part] = contract(head[...], dlogits[:, part], 1, 0)
+            head_back[k, :, part] = contract(head[...], dlogits[:, part], 0, 0)
 
     def make_onehot(k):
         row = lax.broadcasted_iota(jnp.int32, (MISC_ROWS, rows), 0)
@@ -302,14 +458,265 @@
         def _():
             spill_copy(k - 2).wait()
 
+        @pl.when(k == 1)
+        def _():
+            pair_now(1, (1,))
+            need(1, (2, 0))
+            hand_on_now(pass_step >= 2, (2, 0))
+
+        @pl.when(k == 2)
+        def _():
+            need(2, (2, 0))
+            pair_now(3, (2, 0))
+
+        @pl.when(k == 3)
+        def _():
+            need(3, (2, 0))
+
         make_onehot(k)
         tower_forward(k, 0)
+
+        @pl.when(k == 0)
+        def _():
+            pl.when(hops == 3)(chain_on(LATE, False))
+            need_first(LATE)
+            hand_on_now(pass_step == 1, (2, 0))
+
+        @pl.when(k == 1)
+        def _():
+            need(1, (1,))
+            hand_on_now(pass_step >= 2, (1,))
+
+        @pl.when(k == 2)
+        def _():
+            need(2, (1,))
+            pair_now(3, (1,))
+
+        @pl.when(k == 3)
+        def _():
+            need(3, (1,))
+
         tower_forward(k, 1)
-        head_pass(k)
+
+        @pl.when(k == 0)
+        def _():
+            hand_on_now(pass_step == 1, (1,))
+
+        @pl.when(k == 1)
+        def _():
+            pair_now(2, (2, 0))
+
+        def tick():
+            @pl.when(k == 0)
+            def _():
+                pair_now(1, (2, 0))
+
+            @pl.when(k == 1)
+            def _():
+                pair_now(2, (1,))
+
+        head_pass(k, tick)
 
         @pl.when(k < steps - 2)
         def _():
             spill_copy(k).start()
+
+    @pl.when(hops < 3)
+    def _():
+        for n in EARLY + LATE:
+            chain(n).wait_send()
+
+    @pl.when(section != 0)
+    def _():
+        for n in EARLY + LATE:
+            pair(0, n).wait_send()
+        for way in range(2):
+            for n in range(3):
+                give(way, n).wait_send()
+
+    @pl.when(pass_step != 0)
+    def _():
+        for n in range(3):
+            hand_on(n).wait_send()
+
+    for step in range(1, steps):
+        @pl.when(section != step)
+        def _():
+            for n in range(3):
+                pair(step, n).wait_send()
+
+    def lanes(part):
+        return pl.ds(pl.multiple_of(part * LANES, LANES), LANES)
+
+    def core_copy(b, slot, count):
+        return send(
+            sent.at[slot, :, 0:count, lanes(1 - core)], core_in.at[slot, :, 0:count],
+            core_send.at[b], core_recv.at[b], {"dp": mate},
+        )
+
+    def part_copy(b, slot, count, offset):
+        return send(
+            core_sum.at[section_at(offset), 0:count], part_in.at[slot, offset - 1, 0:count],
+            part_send.at[b, offset - 1], part_recv.at[b, offset - 1], {"section": section_at(offset)},
+        )
+
+    def near_rows(count, offset):
+        size = count // near_count
+        return pl.ds(pl.multiple_of(lax.rem(near + offset, near_count) * size, 16), size)
+
+    def near_copy(b, slot, count, offset):
+        return send(
+            part_sum.at[near_rows(count, offset)], near_in.at[slot, offset - 1, 0 : count // near_count],
+            near_send.at[b, offset - 1], near_recv.at[b, offset - 1], {"dp": near_line(offset)},
+        )
+
+    def far_copy(b, slot, count, offset):
+        return send(
+            quarter.at[b, near_rows(count, 0)], far_in.at[slot, offset - 1, 0 : count // near_count],
+            far_send.at[b, offset - 1], far_recv.at[b, offset - 1], {"dp": far_line(offset)},
+        )
+
+    def fill_back(b, count, offset):
+        ref = quarter.at[b, near_rows(count, 0)]
+        return send(ref, ref, fill_send.at[b, offset - 1], fill_recv.at[b, offset - 1], {"dp": near_line(offset)})
+
+    def core_wait(b, slot, count):
+        core_copy(b, slot, count).wait()
+        for j in range(steps):
+            mine = sent[slot, j, 0:count, lanes(core)].astype(F32)
+            core_sum[j, 0:count] = (mine + core_in[slot, j, 0:count].astype(F32)).astype(BF16)
+        for offset in range(1, steps):
+            part_copy(b, slot, count, offset).start()
+
+    def part_wait(b, slot, count):
+        for offset in range(1, steps):
+            part_copy(b, slot, count, offset).wait()
+        total = core_sum[section, 0:count].astype(F32)
+        for n in range(steps - 1):
+            total = total + part_in[slot, n, 0:count].astype(F32)
+        part_sum[0:count] = total.astype(BF16)
+        for offset in range(1, near_count):
+            near_copy(b, slot, count, offset).start()
+
+    def near_wait(b, slot, count):
+        for offset in range(1, near_count):
+            near_copy(b, slot, count, offset).wait()
+        size = count // near_count
+        total = part_sum[near_rows(count, 0)].astype(F32)
+        for n in range(near_count - 1):
+            total = total + near_in[slot, n, 0:size].astype(F32)
+        quarter[b, near_rows(count, 0)] = total.astype(BF16)
+        if far_count > 1:
+            for offset in range(1, far_count):
+                far_copy(b, slot, count, offset).start()
+            for offset in range(1, far_count):
+                far_copy(b, slot, count, offset).wait()
+            for n in range(far_count - 1):
+                total = total + far_in[slot, n, 0:size].astype(F32)
+            quarter[b, near_rows(count, 0)] = total.astype(BF16)
+        for offset in range(1, near_count):
+            fill_back(b, count, offset).start()
+
+    def fill_wait(b, count):
+        for offset in range(1, near_count):
+            fill_back(b, count, offset).wait_send()
+            landed(quarter.at[b, near_rows(count, near_count - offset)], fill_recv.at[b, offset - 1])
+
+    def owner_copy(b, tower, offset):
+        return send(
+            quarter.at[b, 0:QUARTER], whole.at[tower, section], own_send.at[b, offset - 1],
+            own_recv.at[tower, offset - 1], {"section": section_at(steps - offset)},
+        )
+
+    def share_start(b, tower):
+        whole[tower, section] = quarter[b, 0:QUARTER]
+        if tower == 2:
+            for offset in range(1, steps):
+                owner_copy(b, tower, offset).start()
+            return
+        owner = steps - 1 - (b - 1) // 2
+        for offset in range(1, steps):
+            pl.when(lax.rem(section - owner + steps, steps) == offset)(owner_copy(b, tower, offset).start)
+
+    def share_wait(b, tower):
+        def take():
+            for offset in range(1, steps):
+                landed(whole.at[tower, section_at(offset)], own_recv.at[tower, offset - 1])
+            lane_copy(tower).start()
+
+        if tower == 2:
+            for offset in range(1, steps):
+                owner_copy(b, tower, offset).wait_send()
+            take()
+            return
+        owner = steps - 1 - (b - 1) // 2
+        for offset in range(1, steps):
+            pl.when(lax.rem(section - owner + steps, steps) == offset)(owner_copy(b, tower, offset).wait_send)
+        pl.when(section == owner)(take)
+
+    def lane_copy(tower):
+        return send(whole.at[tower], other.at[tower], lane_send.at[tower], lane_recv.at[tower], {"dp": mate})
+
+    def finish(b, tower):
+        def run():
+            lane_copy(tower).wait()
+            for buffer, part in ((whole, core), (other, 1 - core)):
+                for j in range(steps):
+                    values_now = buffer[tower, j].astype(F32) * scale
+                    if tower == 2:
+                        start = j * QUARTER
+                        stop = min(start + QUARTER, head_width)
+                        head_out[start:stop, lanes(part)] = values_now[0 : stop - start]
+                        if stop < start + QUARTER:
+                            at = stop - start
+                            chead_out[:, lanes(part)] = values_now[at : at + chance_count]
+                        continue
+                    size = feat // steps
+                    at = slice(j * size, (j + 1) * size)
+                    entry_out[0, tower, at, lanes(part)] = values_now[0:size]
+                    for m in range(4):
+                        block_out_rows = values_now[(m + 1) * size : (m + 2) * size]
+                        block_out[0, tower, m // 2, m % 2, at, lanes(part)] = block_out_rows
+
+        if tower == 2:
+            run()
+        else:
+            pl.when(section == steps - 1 - (b - 1) // 2)(run)
+
+    def by_kind(b, odd, action):
+        if isinstance(b, int):
+            if 0 <= b <= batches:
+                action(b, 1 if odd else (2 if b == 0 else 0))
+        elif odd:
+            pl.when(b >= 0)(functools.partial(action, b, 1))
+        else:
+            pl.when(b > 0)(functools.partial(action, b, 0))
+            pl.when(b == 0)(functools.partial(action, b, 2))
+
+    def rows_of(b):
+        return LAST if isinstance(b, int) and b == batches else QUARTER
+
+    def fill_and_share(b, tower):
+        fill_wait(b, rows_of(b))
+        share_start(b, tower)
+
+    def ticks(at, parity, turn):
+        if turn == 0:
+            by_kind(at - 2, parity == 1, fill_and_share)
+        elif turn == 1:
+            if not isinstance(at, int) or at <= batches:
+                core_wait(at, parity, rows_of(at))
+        elif turn == 2:
+            if not isinstance(at, int):
+                pl.when(at >= 1)(functools.partial(near_wait, at - 1, 1 - parity, QUARTER))
+            elif at - 1 <= batches:
+                near_wait(at - 1, 1 - parity, rows_of(at - 1))
+        elif turn == 3:
+            by_kind(at - 2, parity == 1, share_wait)
+        else:
+            if not isinstance(at, int) or at <= batches:
+                part_wait(at, parity, rows_of(at))
+            by_kind(at - 3, parity == 0, finish)
 
     def norm_backward(d_out, slope, unit, gain, inverse, at, first):
         d_two = d_out * slope.astype(F32)
@@ -326,10 +733,20 @@
         along = jnp.sum(weighted * gain, axis=0, keepdims=True)
         return ((d_unit - mean - unit * along) * inverse).astype(BF16), d_two
 
-    def tower_backward(k, tower, last):
+    def tower_backward(k, tower, at):
         slot = lax.rem(k, 2)
         act = acts.at[slot, tower]
+        parity = 1 - tower
+        slot_out = tower
+        ticks(at, parity, 0)
         spread_norms(k, tower, False)
+
+        def put(m, value):
+            size = feat // steps
+            for j in range(steps):
+                sent[slot_out, j, m * size : (m + 1) * size] = value[j * size : (j + 1) * size].astype(BF16)
+
+        turn = 1
 
         def norm_of(d_out, at, sub):
             return norm_backward(
@@ -350,21 +767,25 @@
                     d_post, d_two = norm_of(grad[:, sub], outer, sub)
                     prod_a[:, sub] = d_post
                     grad[:, sub] = 0.5 * d_two
+            ticks(at, parity, turn)
+            turn += 1
             for part in chunks:
                 d_mid = contract(weights[k, 5 * tower + 2 + 2 * j], prod_a[:, part], 1, 0)
                 for n, sub in enumerate(subs(part)):
                     d_pre, _ = norm_of(d_mid[:, n * LANES : (n + 1) * LANES], inner, sub)
                     prod_b[:, sub] = d_pre
-            tower_out[k, 5 * tower + 2 + 2 * j] = contract(act[3 + j], prod_a[...], 1, 1)
+            put(2 + 2 * j, contract(act[3 + j], prod_a[...], 1, 1))
             for part in chunks:
                 grad[:, part] += contract(weights[k, 5 * tower + 1 + 2 * j], prod_b[:, part], 1, 0)
-            tower_out[k, 5 * tower + 1 + 2 * j] = contract(act[1 + j], prod_b[...], 1, 1)
+            put(1 + 2 * j, contract(act[1 + j], prod_b[...], 1, 1))
+            ticks(at, parity, turn)
+            turn += 1
         for part in chunks:
             for sub in subs(part):
                 d_first, _ = norm_of(grad[:, sub], 0, sub)
                 prod_a[:, sub] = d_first
         look = lookup(k, tower)
-        tower_out[k, 5 * tower] = contract(act[0], prod_a[...], 1, 1)
+        put(0, contract(act[0], prod_a[...], 1, 1))
         got = contract(onehot[look], prod_a[...], 1, 1)
         if tower == 0:
             misc_grad[k, ACT_ROW : ACT_ROW + action_count] = got[0:action_count]
@@ -377,6 +798,11 @@
             total = contract(ones, acc_dy[n].astype(BF16), 1, 1)
             misc_grad[k, SHIFT_ROW + NORMS * tower + n : SHIFT_ROW + NORMS * tower + n + 1] = 0.5 * total[0:1]
 
+    head_sum[head_width : head_width + chance_count] = chead_sum[...]
+    for j in range(steps):
+        sent[0, j, 0:QUARTER] = head_sum[j * QUARTER : (j + 1) * QUARTER].astype(BF16)
+    core_copy(0, 0, QUARTER).start()
+
     @pl.loop(0, steps)
     def _(back):
         k = steps - 1 - back
@@ -395,12 +821,17 @@
         def _():
             grad[...] = (0.5 * grad[...]).astype(BF16).astype(F32) + head_back[k]
 
-        tower_backward(k, 1, False)
+        tower_backward(k, 1, 2 * back)
+        core_copy(2 * back + 1, 1, QUARTER).start()
         for part in chunks:
             grad[:, part] = contract(weights[k, 5], prod_a[:, part], 1, 0) + contract(
-                chance_head[...], dchance[k, :, part], 1, 0
+                chance_head[...], dchance[k, :, part], 0, 0
             )
-        tower_backward(k, 0, True)
+        tower_backward(k, 0, 2 * back + 1)
+
+        @pl.when(k > 0)
+        def _():
+            core_copy(2 * back + 2, 0, QUARTER).start()
 
         @pl.when(k > 0)
         def _():
@@ -416,31 +847,86 @@
         def _():
             fill_copy(k - 2).start()
 
-    misc_out[...] = misc_grad[...]
-    head_out[...] = head_sum[...]
+    for j in range(steps):
+        sent[0, j, QUARTER:LAST] = misc_grad[j].astype(BF16)
+    core_copy(batches, 0, LAST).start()
+
+    loss_at = [{"dp": mate}] + [{"section": section_at(o)} for o in range(1, steps)]
+    loss_at += [{"dp": near_line(o)} for o in range(1, near_count)]
+    loss_at += [{"dp": far_line(o)} for o in range(1, far_count)]
+    rounds = [1, steps - 1, near_count - 1, far_count - 1]
+    bounds = [sum(rounds[:n]) for n in range(5)]
+
+    def loss_copy(n, stage_at):
+        return send(loss_sum.at[stage_at], loss_in.at[n], loss_send.at[n], loss_recv.at[n], loss_at[n])
+
+    def loss_start(stage_at):
+        for n in range(bounds[stage_at], bounds[stage_at + 1]):
+            loss_copy(n, stage_at).start()
+
+    def loss_wait(stage_at):
+        total = loss_sum[stage_at]
+        for n in range(bounds[stage_at], bounds[stage_at + 1]):
+            loss_copy(n, stage_at).wait()
+            total = total + loss_in[n]
+        loss_sum[stage_at + 1] = total
+
+    def misc_copy():
+        return send(
+            quarter.at[batches, QUARTER:LAST], misc_in.at[0], extra_send.at[0], extra_recv.at[0], {"dp": mate}
+        )
+
+    loss_start(0)
+    for at in range(batches, batches + 4):
+        for turn in range(5):
+            ticks(at, at % 2, turn)
+            if at == batches and turn == 1:
+                loss_wait(0)
+                loss_start(1)
+            if at == batches and turn == 4:
+                loss_wait(1)
+                loss_start(2)
+            if at == batches + 1 and turn == 2:
+                loss_wait(2)
+                loss_start(3)
+            if at == batches + 2 and turn == 0:
+                misc_copy().start()
+    loss_wait(3)
+    loss_out[...] = jnp.sum(loss_sum[4, 0:1], axis=1, keepdims=True) * scale
+    misc_copy().wait()
+    for source, part in ((quarter[batches, QUARTER:LAST], core), (misc_in[0], 1 - core)):
+        got = source.astype(F32) * scale
+        chance_out[0, :, lanes(part)] = got[0:chance_count]
+        action_out[0, :, lanes(part)] = got[ACT_ROW : ACT_ROW + action_count]
+        for tower in range(2):
+            at = GAIN_ROW + tower * NORMS
+            gain_out[0, tower, :, lanes(part)] = got[at : at + NORMS]
+            at = SHIFT_ROW + tower * NORMS
+            shift_out[0, tower, :, lanes(part)] = got[at : at + NORMS]
 
 
 def per_device(
     latent, lengths, actions, chances, value_bins, reward_bins,
     entry_w, action_w, chance_w, block_w, gain_w, shift_w, state_head, chance_head,
 ):
-    full = tuple(
-        lax.all_gather(source, "section", axis=0, tiled=True)
-        for source in (entry_w, block_w, action_w, chance_w, gain_w, shift_w)
-    )
-    steps = full[0].shape[0]
+    steps = lax.axis_size("section")
+    lines = lax.axis_size("dp")
+    near_count = min(4, lines // 2)
+    far_count = lines // 2 // near_count
     rows = latent.shape[0] // steps
     feat = latent.shape[1]
     head_width = state_head.shape[1]
-    head_pad = -(-head_width // LANES) * LANES
-    gains = full[4].reshape(steps, -1, feat)
-    shifts = full[5].reshape(steps, -1, feat)
+    head_pad = steps * QUARTER
+    batches = 2 * steps + 1
     vmem = pl.BlockSpec(memory_space=pltpu.VMEM)
     anys = pl.BlockSpec(memory_space=pl.ANY)
+    dma = pltpu.SemaphoreType.DMA
+    tiny = 1 + (steps - 1) + (near_count - 1) + (far_count - 1)
+    far_slots = max(far_count - 1, 1)
     scratch = [
         pltpu.VMEM((steps, 10, feat, feat), BF16),
         pltpu.VMEM((steps, MISC_ROWS, feat), BF16),
-        pltpu.VMEM((feat, head_pad), BF16),
+        pltpu.VMEM((head_pad, feat), BF16),
         pltpu.VMEM((2, 2, 15, feat, rows), BF16),
         pltpu.VMEM((2 * steps, 8, rows), F32),
         pltpu.VMEM((steps, 8, rows), F32),
@@ -457,52 +943,68 @@
         pltpu.VMEM((head_pad, rows), BF16),
         pltpu.VMEM((steps, 32, rows), BF16),
         pltpu.VMEM((steps, feat, rows), F32),
-        pltpu.VMEM((feat, head_pad + LANES), F32),
+        pltpu.VMEM((head_pad, feat), F32),
+        pltpu.VMEM((32, feat), F32),
         pltpu.VMEM((steps, MISC_ROWS, feat), F32),
+        pltpu.VMEM((5, 8, LANES), F32),
         pltpu.VMEM((steps * WIDE, WIDE), BF16),
         pltpu.VMEM((32, latent.shape[0]), F32),
-        pltpu.SemaphoreType.DMA((steps * 10,)),
-        pltpu.SemaphoreType.DMA((4,)),
+        pltpu.VMEM(latent.shape, BF16),
+        pltpu.VMEM((2, steps, LAST, feat), BF16),
+        pltpu.VMEM((2, steps, LAST, LANES), BF16),
+        pltpu.VMEM((steps, LAST, LANES), BF16),
+        pltpu.VMEM((2, steps - 1, LAST, LANES), BF16),
+        pltpu.VMEM((LAST, LANES), BF16),
+        pltpu.VMEM((2, near_count - 1, LAST // near_count, LANES), BF16),
+        pltpu.VMEM((2, far_slots, LAST // near_count, LANES), BF16),
+        pltpu.VMEM((batches, LAST, LANES), BF16),
+        pltpu.VMEM((3, steps, QUARTER, LANES), BF16),
+        pltpu.VMEM((3, steps, QUARTER, LANES), BF16),
+        pltpu.VMEM((1, MISC_ROWS, LANES), BF16),
+        pltpu.VMEM((tiny, 8, LANES), F32),
+        dma((8,)),
+        dma((4,)),
+        dma((8,)), dma((8,)),
+        dma((2, 3)), dma((steps, 3)), dma((3,)),
+        dma((steps, 8)), dma((steps, 8)),
+        dma((batches,)), dma((batches,)),
+        dma((batches, steps - 1)), dma((batches, steps - 1)),
+        dma((batches, near_count - 1)), dma((batches, near_count - 1)),
+        dma((batches, far_slots)), dma((batches, far_slots)),
+        dma((batches, near_count - 1)), dma((batches, near_count - 1)),
+        dma((batches, steps - 1)), dma((3, steps - 1)),
+        dma((3,)), dma((3,)),
+        dma((1,)), dma((1,)),
+        dma((tiny,)), dma((tiny,)),
     ]
+    scale = 1.0 / (latent.shape[0] * lines)
     outs = pl.pallas_call(
-        kernel,
+        functools.partial(kernel, scale, near_count, far_count),
         out_shape=(
             jax.ShapeDtypeStruct((rows, feat), F32),
-            jax.ShapeDtypeStruct((steps, 10, feat, feat), F32),
-            jax.ShapeDtypeStruct((steps, MISC_ROWS, feat), F32),
-            jax.ShapeDtypeStruct((feat, head_pad + LANES), F32),
-            jax.ShapeDtypeStruct((8, LANES), F32),
+            jax.ShapeDtypeStruct(entry_w.shape, F32),
+            jax.ShapeDtypeStruct(block_w.shape, F32),
+            jax.ShapeDtypeStruct(action_w.shape, F32),
+            jax.ShapeDtypeStruct(chance_w.shape, F32),
+            jax.ShapeDtypeStruct(gain_w.shape, F32),
+            jax.ShapeDtypeStruct(shift_w.shape, F32),
+            jax.ShapeDtypeStruct((head_width, feat), F32),
+            jax.ShapeDtypeStruct((chance_head.shape[1], feat), F32),
+            jax.ShapeDtypeStruct((1, 1), F32),
             jax.ShapeDtypeStruct((steps - 2, 2, 15, feat, rows), BF16),
         ),
-        in_specs=[vmem] * 6 + [anys] * 2 + [vmem] * 6,
-        out_specs=(vmem,) * 5 + (anys,),
+        in_specs=[anys] + [vmem] * 5 + [anys] * 2 + [vmem] * 6,
+        out_specs=(vmem,) * 10 + (anys,),
         scratch_shapes=scratch,
-        compiler_params=pltpu.CompilerParams(vmem_limit_bytes=62 * 2**20),
+        compiler_params=pltpu.CompilerParams(
+            vmem_limit_bytes=63 * 2**20, collective_id=0, has_side_effects=True
+        ),
     )(
         latent, lengths.reshape(1, -1), actions, chances, value_bins, reward_bins,
-        full[0], full[1], full[2], full[3], gains, shifts, state_head, chance_head,
+        entry_w, block_w.reshape(1, 2, 4, feat, feat), action_w, chance_w, gain_w, shift_w,
+        state_head.T, chance_head.T,
     )
-    latent_grad, tower_grad, misc_grad, head_grad, loss, _ = outs
-    tower_grad = lax.psum_scatter(tower_grad.astype(BF16), "section", scatter_dimension=0, tiled=True).astype(F32)
-    misc_grad = lax.psum_scatter(misc_grad, "section", scatter_dimension=0, tiled=True)
-    tower_grad, misc_grad = lax.psum((tower_grad, misc_grad), "dp")
-    head_grad, loss = lax.psum((head_grad, jnp.sum(loss)), ("section", "dp"))
-    scale = 1.0 / (latent.shape[0] * lax.axis_size("dp"))
-    tower_grad = (tower_grad * scale)[0].reshape(2, 5, feat, feat)
-    misc_grad = (misc_grad * scale)[0]
-    act_n = action_w.shape[1]
-    return (
-        latent_grad.reshape(rows, 1, feat),
-        tower_grad[:, 0][None],
-        misc_grad[None, ACT_ROW : ACT_ROW + act_n],
-        misc_grad[None, 0:32],
-        tower_grad[:, 1:].reshape(1, 2, 2, 2, feat, feat),
-        misc_grad[GAIN_ROW : GAIN_ROW + 10].reshape(1, 2, 5, feat),
-        misc_grad[SHIFT_ROW : SHIFT_ROW + 10].reshape(1, 2, 5, feat),
-        head_grad[:, :head_width] * scale,
-        head_grad[:, head_pad : head_pad + 32] * scale,
-        loss * scale,
-    )
+    return (outs[0].reshape(rows, 1, feat), outs[1], outs[3], outs[4], outs[2], outs[5], outs[6]) + (outs[7].T, outs[8].T, outs[9].reshape(()))
 
 
 def solution(mesh):

time: 554 us -> 217 us (0.39)
  waiting for transfers between devices: 270 us -> 0 us
  blocking collectives: 139 us -> 0 us
  Pallas kernels: 103 us -> 199 us
  between operations: 16 us -> 2.44 us
  other arithmetic: 11.1 us -> 0 us
    psum x2 -> x0, waiting for transfers between devices: 139 us -> none  [the longest x1 133 us: per_device(): head_grad, loss = lax.psum((head_grad, jnp.sum(loss)), ('section', 'dp'))]
    psum x2 -> x0, blocking collectives: 105 us -> none  [the longest x1 65.6 us: per_device(): tower_grad, misc_grad = lax.psum((tower_grad, misc_grad), 'dp')]
    pallas_call x1, Pallas kernels: 103 us -> 199 us  [per_device(): pl.pallas_call(functools.partial(kernel, scale, near_count, far_count), o...]
    unnamed x8 -> x0, waiting for transfers between devices: 84.9 us -> none
    all_gather x2 -> x0, waiting for transfers between devices: 46.1 us -> none  [per_device(): lax.all_gather(source, 'section', axis=0, tiled=True)]
    all_gather x4 -> x0, blocking collectives: 34.3 us -> none  [per_device(): lax.all_gather(source, 'section', axis=0, tiled=True)]
    convert_element_type x1 -> x0, other arithmetic: 6.99 us -> none  [per_device(): tower_grad.astype(BF16)]
    unnamed x15 -> x21, local copies, waits for them, and re-layouts: 9.27 us -> 15 us
  transfers between devices with their start and end apart: 6 -> 0, of which waited for: 5 -> 0; matrix products, arithmetic and copies ran while one was open for 4% -> 0% of each run, Pallas kernels for 0% -> 0%
where the time goes in v2:
time: 217 us
  Pallas kernels  199 us (92%)
  local copies, waits for them, and re-layouts  15 us (7%)
  between operations  2.44 us (1%)
    pallas_call x1, Pallas kernels, per_device(): pl.pallas_call(functools.partial(kernel, scale, near_count, far_count), o...  199 us
    unnamed x21, local copies, waits for them, and re-layouts  15 us

profile of v2, /device:TPU:0, one launch (start us, length us, event | category | flops | bytes accessed | tf_op | source)
XLA Modules:
  0.0 216.6 jit_solution(5204374810310729518)
XLA Ops:
  0.6 1.3 copy.24.gains
  1.9 1.3 copy.25.shifts
  3.2 199.2 %shard_map.213 = (f32[768,256]{1,0:T(8,128)}, f32[1,2,256,256]{3,2,1,0:T(8,128)}, f32[1,2,2,2,256,256]{5,4,3,2,1,0:T(8,128)}, f32[1,4,256]{2,1,0:T(4,128)}, f32[...) custom-call(bf16[3072,256]{1,0:T(8,128)(2,1)} %latent.1, ...), custom_call_target="tpu_custom_call" | custom-call | tf_op jit(solution)/shard_map/pallas_call | solution.py:981
  202.5 0.0 copy-start.4
  202.5 0.0 copy-start.3
  202.5 0.0 copy-start
  202.5 3.0 %copy.26 = f32[768,1,256]{2,1,0:T(1,128)} copy(f32[768,1,256]{2,0,1:T(8,128)} %bitcast.10) | data formatting | bytes 1572864
  205.5 1.3 copy.27
  206.8 1.3 copy.28
  208.1 1.9 copy.36
  210.0 0.0 copy-done.4
  210.0 0.6 copy.37
  210.6 0.0 copy-done.3
  210.6 0.6 copy.38
  211.2 0.0 copy-done
  211.2 0.0 copy-start.1
  211.2 1.3 copy.39
  212.5 0.7 copy-done.1
  213.2 0.0 copy-start.2
  213.2 1.0 copy.40
  214.3 0.0 copy-done.2
  214.3 0.6 copy.41
Async XLA Ops:
  202.5 7.5 %copy-start.4 = (f32[1,4,256]{2,1,0:T(4,128)S(1)}, f32[1,4,256]{2,1,0:T(4,128)}, u32[]{:S(2)}) copy-start(f32[1,4,256]{2,1,0:T(4,128)} %get-tuple-element.52) | copy-start | bytes 12292
  202.5 8.1 %copy-start.3 = (f32[1,32,256]{2,1,0:T(8,128)S(1)}, f32[1,32,256]{2,1,0:T(8,128)}, u32[]{:S(2)}) copy-start(f32[1,32,256]{2,1,0:T(8,128)} %get-tuple-element.53) | copy-start | bytes 98308
  202.5 8.7 %copy-start = (f32[1,2,2,2,256,256]{5,4,3,2,1,0:T(8,128)S(1)}, f32[1,2,2,2,256,256]{5,4,3,2,1,0:T(8,128)}, u32[]{:S(2)}) copy-start(f32[1,2,2,2,256,256]{5,4,3,2,1,0:T(8,128)} %get-tuple-element.54) | copy-start | bytes 6291460
  211.2 2.0 copy-start.1
  213.2 1.0 copy-start.2

commit v3 on v2

--- a/solution.py
+++ b/solution.py
@@ -29,31 +29,22 @@
 
 
 def gelu_pair(half):
-    square = half * half * K2
-    inner = half * (square + K1)
+    inner = half * (half * half * K2 + K1)
     plus = jnp.tanh(inner) + 1.0
-    slope = half * (square * 3.0 + K1)
-    return half * plus, plus * ((2.0 - plus) * slope + 1.0)
-
-
-def norm_forward(values, gain, shift, residual):
-    feature_count = values.shape[0]
-    center = values - jnp.sum(values, axis=0, keepdims=True) * (1.0 / feature_count)
-    inverse = lax.rsqrt(jnp.sum(center * center, axis=0, keepdims=True) + feature_count * EPS)
-    unit = center * inverse
-    half = unit * gain + shift
-    if residual is not None:
-        half = half + 0.5 * residual
-    out, slope = gelu_pair(half)
-    return out, slope, unit, inverse
-
-
+    out = half * plus
+    slope = inner * 3.0 - half * (2.0 * K1)
+    return out, (plus * ((2.0 - plus) * slope + 1.0)).astype(BF16)
+
+
+BAND = 32
 QUARTER = 320
 LAST = 384
 CHAIN = ((0, 1), (1, 2), (2, 3), (3, 4), (4, 6), (6, 8), (8, 10))
 EARLY = (7, 0, 1, 2, 3, 4)
 LATE = (5, 6)
 MESH = pl.DeviceIdType.MESH
+TICK_AT = 1
+PART_LAG, NEAR_LAG, FILL_LAG, OWN_LAG, DONE_LAG = 2, 4, 6, 9, 10
 
 
 def when(condition, action):
@@ -68,10 +59,10 @@
     scale, near_count, far_count,
     latent, lengths, actions, chances, values, rewards, entry, blocks, action_w, chance_w, gains, shifts,
     state_head, chance_head,
-    latent_out, entry_out, block_out, action_out, chance_out, gain_out, shift_out, head_out, chead_out, loss_out, spill,
+    latent_out, both, misc_both, loss_out, spill,
     weights, misc, head, acts, inv, ids, onehot, current, resid, prod_a, prod_b, grad, gb, acc_dy, acc_p,
     logits, dlogits, dchance, head_back, head_sum, chead_sum, misc_grad, loss_sum, sel, stage, states,
-    sent, core_in, core_sum, part_in, part_sum, near_in, far_in, quarter, whole, other, misc_in, loss_in,
+    sent, core_in, core_sum, part_in, part_sum, near_in, far_in, quarter, loss_in,
     load_sem, spill_sem, chain_send, chain_recv, give_send, step_recv, pass_send, pair_send, pair_recv,
     core_send, core_recv, part_send, part_recv, near_send, near_recv, far_send, far_recv,
     fill_send, fill_recv, own_send, own_recv, lane_send, lane_recv, extra_send, extra_recv, loss_send, loss_recv,
@@ -126,10 +117,10 @@
         [
             chance_w[0].astype(F32),
             action_w[0].astype(F32),
-            gains[0, 0].astype(F32),
-            gains[0, 1].astype(F32),
-            shifts[0, 0].astype(F32),
-            shifts[0, 1].astype(F32),
+            gains[0, :, 0].astype(F32),
+            gains[0, :, 1].astype(F32),
+            shifts[0, :, 0].astype(F32),
+            shifts[0, :, 1].astype(F32),
             jnp.zeros((MISC_ROWS - SHIFT_ROW - 2 * NORMS, feat), F32),
         ],
         axis=0,
@@ -270,11 +261,12 @@
     loss_sum[...] = jnp.zeros_like(loss_sum)
 
     pl.when((hops == 1) | (hops == 2))(chain_on(EARLY + LATE, True))
-    pl.when(section == 1)(give_now(1))
-    pl.when(section == 2)(give_now(0))
-    pl.when(section == 3)(give_now(0))
+    pl.when(hops == 3)(chain_on(EARLY[:4], False))
+    pl.when((section == 1) & (core == 1))(give_now(1))
+    pl.when((section == 2) & (core == 1))(give_now(0))
     pl.when(section == 3)(give_now(1))
-    pl.when(hops == 3)(chain_on(EARLY, False))
+    pl.when(hops == 3)(chain_on(EARLY[4:], False))
+    pl.when((section == 2) & (core == 0))(give_now(0))
     need_first(EARLY)
 
     def spread_norms(k, tower, with_shift):
@@ -287,11 +279,11 @@
         pick = pick + jnp.where((at >= NORMS) & (row == shift_row + at - NORMS), 0.5, 0.0)
         gb[:, 0 : count * LANES] = contract(misc[k], pick.astype(BF16), 0, 0)
 
-    def gain_of(n):
-        return gb[:, n * LANES : (n + 1) * LANES]
-
-    def shift_of(n):
-        return gb[:, (NORMS + n) * LANES : (NORMS + n + 1) * LANES]
+    def gain_of(n, band=slice(None)):
+        return gb[band, n * LANES : (n + 1) * LANES]
+
+    def shift_of(n, band=slice(None)):
+        return gb[band, (NORMS + n) * LANES : (NORMS + n + 1) * LANES]
 
     def lookup(k, tower):
         lo = ACT_ROW if tower == 0 else 0
@@ -303,45 +295,39 @@
         spread_norms(k, tower, True)
         act[0] = current[...]
         look = lookup(k, tower)
-        for part in chunks:
-            first = contract(weights[k, 5 * tower], act[0, :, part], 0, 0)
-            first = first + contract(misc[k, look], onehot[look, part], 0, 0)
-            for n, sub in enumerate(subs(part)):
-                out, slope, unit, inverse = norm_forward(
-                    first[:, n * LANES : (n + 1) * LANES], gain_of(0), shift_of(0), None
-                )
-                resid[:, sub] = out
-                act[1, :, sub] = out.astype(BF16)
-                act[5, :, sub] = unit.astype(BF16)
-                act[10, :, sub] = slope.astype(BF16)
-                inv[2 * k + tower, 0:1, sub] = inverse
-        for j in range(2):
+
+        def multiply(n, part):
+            matrix = weights[k, 5 * tower + n]
+            if n == 0:
+                got = contract(matrix, act[0, :, part], 0, 0)
+                return got + contract(misc[k, look], onehot[look, part], 0, 0)
+            return contract(matrix, act[1 + n // 2 if n % 2 == 1 else 2 + n // 2, :, part], 0, 0)
+
+        def apply(n, sub, values):
+            values = values - jnp.sum(values, axis=0, keepdims=True) * (1.0 / feat)
+            inverse = lax.rsqrt(jnp.sum(values * values, axis=0, keepdims=True) + feat * EPS)
+            inv[2 * k + tower, n : n + 1, sub] = inverse
+            for r in range(0, feat, BAND):
+                band = slice(r, r + BAND)
+                unit = values[band] * inverse
+                half = unit * gain_of(n, band) + shift_of(n, band)
+                if n > 0 and n % 2 == 0:
+                    half = half + 0.5 * resid[band, sub]
+                out, slope = gelu_pair(half)
+                if n == 0 or n == 2:
+                    resid[band, sub] = out
+                if n == 4:
+                    current[band, sub] = out.astype(BF16)
+                else:
+                    act[1 + n // 2 if n % 2 == 0 else 3 + n // 2, band, sub] = out.astype(BF16)
+                act[5 + n, band, sub] = unit.astype(BF16)
+                act[10 + n, band, sub] = slope
+
+        for n in range(NORMS):
             for part in chunks:
-                pre = contract(weights[k, 5 * tower + 1 + 2 * j], act[1 + j, :, part], 0, 0)
-                for n, sub in enumerate(subs(part)):
-                    at = 1 + 2 * j
-                    out, slope, unit, inverse = norm_forward(
-                        pre[:, n * LANES : (n + 1) * LANES], gain_of(at), shift_of(at), None
-                    )
-                    act[3 + j, :, sub] = out.astype(BF16)
-                    act[5 + at, :, sub] = unit.astype(BF16)
-                    act[10 + at, :, sub] = slope.astype(BF16)
-                    inv[2 * k + tower, at : at + 1, sub] = inverse
-            for part in chunks:
-                post = contract(weights[k, 5 * tower + 2 + 2 * j], act[3 + j, :, part], 0, 0)
-                for n, sub in enumerate(subs(part)):
-                    at = 2 + 2 * j
-                    out, slope, unit, inverse = norm_forward(
-                        post[:, n * LANES : (n + 1) * LANES], gain_of(at), shift_of(at), resid[:, sub]
-                    )
-                    if j == 0:
-                        resid[:, sub] = out
-                        act[2, :, sub] = out.astype(BF16)
-                    else:
-                        current[:, sub] = out.astype(BF16)
-                    act[5 + at, :, sub] = unit.astype(BF16)
-                    act[10 + at, :, sub] = slope.astype(BF16)
-                    inv[2 * k + tower, at : at + 1, sub] = inverse
+                values = multiply(n, part)
+                for c, sub in enumerate(subs(part)):
+                    apply(n, sub, values[:, c * LANES : (c + 1) * LANES])
 
     def softmax_block(pieces, target, live):
         top = None
@@ -460,14 +446,12 @@
 
         @pl.when(k == 1)
         def _():
-            pair_now(1, (1,))
             need(1, (2, 0))
-            hand_on_now(pass_step >= 2, (2, 0))
+            hand_on_now(pass_step == 2, (2, 0))
 
         @pl.when(k == 2)
         def _():
             need(2, (2, 0))
-            pair_now(3, (2, 0))
 
         @pl.when(k == 3)
         def _():
@@ -480,20 +464,23 @@
         def _():
             pl.when(hops == 3)(chain_on(LATE, False))
             need_first(LATE)
+            pl.when((section == 1) & (core == 0))(give_now(1))
             hand_on_now(pass_step == 1, (2, 0))
 
         @pl.when(k == 1)
         def _():
+            pair_now(1, (1,))
+            hand_on_now(pass_step == 2, (1,))
             need(1, (1,))
-            hand_on_now(pass_step >= 2, (1,))
 
         @pl.when(k == 2)
         def _():
+            hand_on_now(pass_step == 3, (1,))
             need(2, (1,))
+
+        @pl.when(k == 3)
+        def _():
             pair_now(3, (1,))
-
-        @pl.when(k == 3)
-        def _():
             need(3, (1,))
 
         tower_forward(k, 1)
@@ -501,6 +488,7 @@
         @pl.when(k == 0)
         def _():
             hand_on_now(pass_step == 1, (1,))
+            pl.when(section == 3)(give_now(0))
 
         @pl.when(k == 1)
         def _():
@@ -514,6 +502,11 @@
             @pl.when(k == 1)
             def _():
                 pair_now(2, (1,))
+                hand_on_now(pass_step == 3, (2, 0))
+
+            @pl.when(k == 2)
+            def _():
+                pair_now(3, (2, 0))
 
         head_pass(k, tick)
 
@@ -556,7 +549,7 @@
 
     def part_copy(b, slot, count, offset):
         return send(
-            core_sum.at[section_at(offset), 0:count], part_in.at[slot, offset - 1, 0:count],
+            core_sum.at[slot, section_at(offset), 0:count], part_in.at[b, offset - 1, 0:count],
             part_send.at[b, offset - 1], part_recv.at[b, offset - 1], {"section": section_at(offset)},
         )
 
@@ -566,13 +559,13 @@
 
     def near_copy(b, slot, count, offset):
         return send(
-            part_sum.at[near_rows(count, offset)], near_in.at[slot, offset - 1, 0 : count // near_count],
+            part_sum.at[slot, near_rows(count, offset)], near_in.at[b, offset - 1, 0 : count // near_count],
             near_send.at[b, offset - 1], near_recv.at[b, offset - 1], {"dp": near_line(offset)},
         )
 
     def far_copy(b, slot, count, offset):
         return send(
-            quarter.at[b, near_rows(count, 0)], far_in.at[slot, offset - 1, 0 : count // near_count],
+            quarter.at[b, near_rows(count, 0)], far_in.at[b, offset - 1, 0 : count // near_count],
             far_send.at[b, offset - 1], far_recv.at[b, offset - 1], {"dp": far_line(offset)},
         )
 
@@ -584,17 +577,17 @@
         core_copy(b, slot, count).wait()
         for j in range(steps):
             mine = sent[slot, j, 0:count, lanes(core)].astype(F32)
-            core_sum[j, 0:count] = (mine + core_in[slot, j, 0:count].astype(F32)).astype(BF16)
+            core_sum[slot, j, 0:count] = (mine + core_in[slot, j, 0:count].astype(F32)).astype(BF16)
         for offset in range(1, steps):
             part_copy(b, slot, count, offset).start()
 
     def part_wait(b, slot, count):
         for offset in range(1, steps):
             part_copy(b, slot, count, offset).wait()
-        total = core_sum[section, 0:count].astype(F32)
+        total = core_sum[slot, section, 0:count].astype(F32)
         for n in range(steps - 1):
-            total = total + part_in[slot, n, 0:count].astype(F32)
-        part_sum[0:count] = total.astype(BF16)
+            total = total + part_in[b, n, 0:count].astype(F32)
+        part_sum[slot, 0:count] = total.astype(BF16)
         for offset in range(1, near_count):
             near_copy(b, slot, count, offset).start()
 
@@ -602,9 +595,9 @@
         for offset in range(1, near_count):
             near_copy(b, slot, count, offset).wait()
         size = count // near_count
-        total = part_sum[near_rows(count, 0)].astype(F32)
+        total = part_sum[slot, near_rows(count, 0)].astype(F32)
         for n in range(near_count - 1):
-            total = total + near_in[slot, n, 0:size].astype(F32)
+            total = total + near_in[b, n, 0:size].astype(F32)
         quarter[b, near_rows(count, 0)] = total.astype(BF16)
         if far_count > 1:
             for offset in range(1, far_count):
@@ -612,7 +605,7 @@
             for offset in range(1, far_count):
                 far_copy(b, slot, count, offset).wait()
             for n in range(far_count - 1):
-                total = total + far_in[slot, n, 0:size].astype(F32)
+                total = total + far_in[b, n, 0:size].astype(F32)
             quarter[b, near_rows(count, 0)] = total.astype(BF16)
         for offset in range(1, near_count):
             fill_back(b, count, offset).start()
@@ -624,24 +617,28 @@
 
     def owner_copy(b, tower, offset):
         return send(
-            quarter.at[b, 0:QUARTER], whole.at[tower, section], own_send.at[b, offset - 1],
+            quarter.at[b, 0:QUARTER], both.at[core, tower, section], own_send.at[b, offset - 1],
             own_recv.at[tower, offset - 1], {"section": section_at(steps - offset)},
         )
 
     def share_start(b, tower):
-        whole[tower, section] = quarter[b, 0:QUARTER]
+        def keep():
+            both[core, tower, section] = quarter[b, 0:QUARTER]
+
         if tower == 2:
+            keep()
             for offset in range(1, steps):
                 owner_copy(b, tower, offset).start()
             return
         owner = steps - 1 - (b - 1) // 2
+        pl.when(section == owner)(keep)
         for offset in range(1, steps):
             pl.when(lax.rem(section - owner + steps, steps) == offset)(owner_copy(b, tower, offset).start)
 
     def share_wait(b, tower):
         def take():
             for offset in range(1, steps):
-                landed(whole.at[tower, section_at(offset)], own_recv.at[tower, offset - 1])
+                landed(both.at[core, tower, section_at(offset)], own_recv.at[tower, offset - 1])
             lane_copy(tower).start()
 
         if tower == 2:
@@ -655,28 +652,13 @@
         pl.when(section == owner)(take)
 
     def lane_copy(tower):
-        return send(whole.at[tower], other.at[tower], lane_send.at[tower], lane_recv.at[tower], {"dp": mate})
+        ref = both.at[core, tower]
+        return send(ref, ref, lane_send.at[tower], lane_recv.at[tower], {"dp": mate})
 
     def finish(b, tower):
         def run():
-            lane_copy(tower).wait()
-            for buffer, part in ((whole, core), (other, 1 - core)):
-                for j in range(steps):
-                    values_now = buffer[tower, j].astype(F32) * scale
-                    if tower == 2:
-                        start = j * QUARTER
-                        stop = min(start + QUARTER, head_width)
-                        head_out[start:stop, lanes(part)] = values_now[0 : stop - start]
-                        if stop < start + QUARTER:
-                            at = stop - start
-                            chead_out[:, lanes(part)] = values_now[at : at + chance_count]
-                        continue
-                    size = feat // steps
-                    at = slice(j * size, (j + 1) * size)
-                    entry_out[0, tower, at, lanes(part)] = values_now[0:size]
-                    for m in range(4):
-                        block_out_rows = values_now[(m + 1) * size : (m + 2) * size]
-                        block_out[0, tower, m // 2, m % 2, at, lanes(part)] = block_out_rows
+            lane_copy(tower).wait_send()
+            landed(both.at[1 - core, tower], lane_recv.at[tower])
 
         if tower == 2:
             run()
@@ -700,23 +682,26 @@
         fill_wait(b, rows_of(b))
         share_start(b, tower)
 
-    def ticks(at, parity, turn):
-        if turn == 0:
-            by_kind(at - 2, parity == 1, fill_and_share)
-        elif turn == 1:
-            if not isinstance(at, int) or at <= batches:
+    def ticks(at, parity):
+        inside = not isinstance(at, int)
+
+        def odd(lag):
+            return (parity + lag) % 2 == 1
+
+        by_kind(at - DONE_LAG, odd(DONE_LAG), finish)
+        by_kind(at - OWN_LAG, odd(OWN_LAG), share_wait)
+        by_kind(at - FILL_LAG, odd(FILL_LAG), fill_and_share)
+        if inside:
+            pl.when(at >= NEAR_LAG)(functools.partial(near_wait, at - NEAR_LAG, parity, QUARTER))
+            pl.when(at >= PART_LAG)(functools.partial(part_wait, at - PART_LAG, parity, QUARTER))
+            core_wait(at, parity, QUARTER)
+        else:
+            if at - NEAR_LAG <= batches:
+                near_wait(at - NEAR_LAG, parity, rows_of(at - NEAR_LAG))
+            if at - PART_LAG <= batches:
+                part_wait(at - PART_LAG, parity, rows_of(at - PART_LAG))
+            if at <= batches:
                 core_wait(at, parity, rows_of(at))
-        elif turn == 2:
-            if not isinstance(at, int):
-                pl.when(at >= 1)(functools.partial(near_wait, at - 1, 1 - parity, QUARTER))
-            elif at - 1 <= batches:
-                near_wait(at - 1, 1 - parity, rows_of(at - 1))
-        elif turn == 3:
-            by_kind(at - 2, parity == 1, share_wait)
-        else:
-            if not isinstance(at, int) or at <= batches:
-                part_wait(at, parity, rows_of(at))
-            by_kind(at - 3, parity == 0, finish)
 
     def norm_backward(d_out, slope, unit, gain, inverse, at, first):
         d_two = d_out * slope.astype(F32)
@@ -736,9 +721,7 @@
     def tower_backward(k, tower, at):
         slot = lax.rem(k, 2)
         act = acts.at[slot, tower]
-        parity = 1 - tower
         slot_out = tower
-        ticks(at, parity, 0)
         spread_norms(k, tower, False)
 
         def put(m, value):
@@ -746,7 +729,6 @@
             for j in range(steps):
                 sent[slot_out, j, m * size : (m + 1) * size] = value[j * size : (j + 1) * size].astype(BF16)
 
-        turn = 1
 
         def norm_of(d_out, at, sub):
             return norm_backward(
@@ -767,8 +749,8 @@
                     d_post, d_two = norm_of(grad[:, sub], outer, sub)
                     prod_a[:, sub] = d_post
                     grad[:, sub] = 0.5 * d_two
-            ticks(at, parity, turn)
-            turn += 1
+            if j == TICK_AT:
+                ticks(at, 1 - tower)
             for part in chunks:
                 d_mid = contract(weights[k, 5 * tower + 2 + 2 * j], prod_a[:, part], 1, 0)
                 for n, sub in enumerate(subs(part)):
@@ -778,8 +760,6 @@
             for part in chunks:
                 grad[:, part] += contract(weights[k, 5 * tower + 1 + 2 * j], prod_b[:, part], 1, 0)
             put(1 + 2 * j, contract(act[1 + j], prod_b[...], 1, 1))
-            ticks(at, parity, turn)
-            turn += 1
         for part in chunks:
             for sub in subs(part):
                 d_first, _ = norm_of(grad[:, sub], 0, sub)
@@ -873,36 +853,58 @@
 
     def misc_copy():
         return send(
-            quarter.at[batches, QUARTER:LAST], misc_in.at[0], extra_send.at[0], extra_recv.at[0], {"dp": mate}
+            quarter.at[batches, QUARTER:LAST], misc_both.at[core], extra_send.at[0], extra_recv.at[0], {"dp": mate}
         )
 
     loss_start(0)
-    for at in range(batches, batches + 4):
-        for turn in range(5):
-            ticks(at, at % 2, turn)
-            if at == batches and turn == 1:
-                loss_wait(0)
-                loss_start(1)
-            if at == batches and turn == 4:
-                loss_wait(1)
-                loss_start(2)
-            if at == batches + 1 and turn == 2:
-                loss_wait(2)
-                loss_start(3)
-            if at == batches + 2 and turn == 0:
-                misc_copy().start()
+    for at in range(batches, batches + DONE_LAG + 1):
+        ticks(at, at % 2)
+        if at < batches + 3:
+            loss_wait(at - batches)
+            loss_start(at - batches + 1)
+        if at == batches + FILL_LAG:
+            misc_copy().start()
     loss_wait(3)
     loss_out[...] = jnp.sum(loss_sum[4, 0:1], axis=1, keepdims=True) * scale
-    misc_copy().wait()
-    for source, part in ((quarter[batches, QUARTER:LAST], core), (misc_in[0], 1 - core)):
-        got = source.astype(F32) * scale
-        chance_out[0, :, lanes(part)] = got[0:chance_count]
-        action_out[0, :, lanes(part)] = got[ACT_ROW : ACT_ROW + action_count]
+    misc_both[core] = quarter[batches, QUARTER:LAST]
+    misc_copy().wait_send()
+    landed(misc_both.at[1 - core], extra_recv.at[0])
+
+
+def finish_kernel(
+    scale, latent_in, both, misc_both,
+    latent_out, entry_out, block_out, action_out, chance_out, gain_out, shift_out, head_out, chead_out,
+):
+    steps = both.shape[2]
+    feat = entry_out.shape[-1]
+    size = feat // steps
+    head_width = head_out.shape[0]
+    chance_count = chead_out.shape[0]
+    latent_out[:, 0, :] = latent_in[...]
+    for part in range(2):
+        lanes = slice(part * LANES, (part + 1) * LANES)
+        for j in range(steps):
+            at = slice(j * size, (j + 1) * size)
+            for tower in range(2):
+                got = both[part, tower, j].astype(F32) * scale
+                entry_out[0, tower, at, lanes] = got[0:size]
+                for m in range(4):
+                    block_out[0, tower, m // 2, m % 2, at, lanes] = got[(m + 1) * size : (m + 2) * size]
+            got = both[part, 2, j].astype(F32) * scale
+            start = j * QUARTER
+            stop = min(start + QUARTER, head_width)
+            head_out[start:stop, lanes] = got[0 : stop - start]
+            if stop < start + QUARTER:
+                chead_out[:, lanes] = got[stop - start : stop - start + chance_count]
+        got = misc_both[part].astype(F32) * scale
+        chance_out[0, :, lanes] = got[0:chance_count]
+        action_out[0, :, lanes] = got[ACT_ROW : ACT_ROW + action_out.shape[1]]
         for tower in range(2):
-            at = GAIN_ROW + tower * NORMS
-            gain_out[0, tower, :, lanes(part)] = got[at : at + NORMS]
-            at = SHIFT_ROW + tower * NORMS
-            shift_out[0, tower, :, lanes(part)] = got[at : at + NORMS]
+            for n in range(NORMS):
+                at = GAIN_ROW + tower * NORMS + n
+                gain_out[0, n, tower : tower + 1, lanes] = got[at : at + 1]
+                at = SHIFT_ROW + tower * NORMS + n
+                shift_out[0, n, tower : tower + 1, lanes] = got[at : at + 1]
 
 
 def per_device(
@@ -952,15 +954,12 @@
         pltpu.VMEM(latent.shape, BF16),
         pltpu.VMEM((2, steps, LAST, feat), BF16),
         pltpu.VMEM((2, steps, LAST, LANES), BF16),
-        pltpu.VMEM((steps, LAST, LANES), BF16),
-        pltpu.VMEM((2, steps - 1, LAST, LANES), BF16),
-        pltpu.VMEM((LAST, LANES), BF16),
-        pltpu.VMEM((2, near_count - 1, LAST // near_count, LANES), BF16),
-        pltpu.VMEM((2, far_slots, LAST // near_count, LANES), BF16),
+        pltpu.VMEM((2, steps, LAST, LANES), BF16),
+        pltpu.VMEM((batches, steps - 1, LAST, LANES), BF16),
+        pltpu.VMEM((2, LAST, LANES), BF16),
+        pltpu.VMEM((batches, near_count - 1, LAST // near_count, LANES), BF16),
+        pltpu.VMEM((batches, far_slots, LAST // near_count, LANES), BF16),
         pltpu.VMEM((batches, LAST, LANES), BF16),
-        pltpu.VMEM((3, steps, QUARTER, LANES), BF16),
-        pltpu.VMEM((3, steps, QUARTER, LANES), BF16),
-        pltpu.VMEM((1, MISC_ROWS, LANES), BF16),
         pltpu.VMEM((tiny, 8, LANES), F32),
         dma((8,)),
         dma((4,)),
@@ -982,29 +981,46 @@
         functools.partial(kernel, scale, near_count, far_count),
         out_shape=(
             jax.ShapeDtypeStruct((rows, feat), F32),
-            jax.ShapeDtypeStruct(entry_w.shape, F32),
-            jax.ShapeDtypeStruct(block_w.shape, F32),
-            jax.ShapeDtypeStruct(action_w.shape, F32),
-            jax.ShapeDtypeStruct(chance_w.shape, F32),
-            jax.ShapeDtypeStruct(gain_w.shape, F32),
-            jax.ShapeDtypeStruct(shift_w.shape, F32),
-            jax.ShapeDtypeStruct((head_width, feat), F32),
-            jax.ShapeDtypeStruct((chance_head.shape[1], feat), F32),
+            jax.ShapeDtypeStruct((2, 3, steps, QUARTER, LANES), BF16),
+            jax.ShapeDtypeStruct((2, MISC_ROWS, LANES), BF16),
             jax.ShapeDtypeStruct((1, 1), F32),
             jax.ShapeDtypeStruct((steps - 2, 2, 15, feat, rows), BF16),
         ),
         in_specs=[anys] + [vmem] * 5 + [anys] * 2 + [vmem] * 6,
-        out_specs=(vmem,) * 10 + (anys,),
+        out_specs=(vmem,) * 4 + (anys,),
         scratch_shapes=scratch,
         compiler_params=pltpu.CompilerParams(
             vmem_limit_bytes=63 * 2**20, collective_id=0, has_side_effects=True
         ),
     )(
         latent, lengths.reshape(1, -1), actions, chances, value_bins, reward_bins,
-        entry_w, block_w.reshape(1, 2, 4, feat, feat), action_w, chance_w, gain_w, shift_w,
-        state_head.T, chance_head.T,
+        entry_w, block_w.reshape(1, 2, 4, feat, feat), action_w, chance_w,
+        jnp.swapaxes(gain_w, 1, 2), jnp.swapaxes(shift_w, 1, 2), state_head.T, chance_head.T,
     )
-    return (outs[0].reshape(rows, 1, feat), outs[1], outs[3], outs[4], outs[2], outs[5], outs[6]) + (outs[7].T, outs[8].T, outs[9].reshape(()))
+    swapped = (1, gain_w.shape[2], gain_w.shape[1], feat)
+    done = pl.pallas_call(
+        functools.partial(finish_kernel, scale),
+        out_shape=(
+            jax.ShapeDtypeStruct((rows, 1, feat), F32),
+            jax.ShapeDtypeStruct(entry_w.shape, F32),
+            jax.ShapeDtypeStruct(block_w.shape, F32),
+            jax.ShapeDtypeStruct(action_w.shape, F32),
+            jax.ShapeDtypeStruct(chance_w.shape, F32),
+            jax.ShapeDtypeStruct(swapped, F32),
+            jax.ShapeDtypeStruct(swapped, F32),
+            jax.ShapeDtypeStruct((head_width, feat), F32),
+            jax.ShapeDtypeStruct((chance_head.shape[1], feat), F32),
+        ),
+        in_specs=[vmem] * 3,
+        out_specs=(vmem,) * 9,
+        compiler_params=pltpu.CompilerParams(vmem_limit_bytes=32 * 2**20),
+    )(outs[0], outs[1], outs[2])
+    latent_grad, entry_grad, block_grad, action_grad, chance_grad, gain_grad, shift_grad, head_grad, chead_grad = done
+    return (
+        latent_grad, entry_grad, action_grad, chance_grad, block_grad,
+        jnp.swapaxes(gain_grad, 1, 2), jnp.swapaxes(shift_grad, 1, 2),
+        head_grad.T, chead_grad.T, outs[3].reshape(()),
+    )
 
 
 def solution(mesh):

time: 217 us -> 163 us (0.75)
  Pallas kernels: 199 us -> 157 us
  local copies, waits for them, and re-layouts: 15 us -> 3.43 us
    pallas_call x1, Pallas kernels: 199 us -> 154 us  [per_device(): pl.pallas_call(functools.partial(kernel, scale, near_count, far_count), o...]
    unnamed x21 -> x6, local copies, waits for them, and re-layouts: 15 us -> 3.43 us
    pallas_call x0 -> x1, Pallas kernels: none -> 2.32 us  [per_device(): pl.pallas_call(functools.partial(finish_kernel, scale), out_shape=(jax.Sh...]
where the time goes in v3:
time: 163 us; the launch traced here: 162 us
  Pallas kernels  157 us (96%)
  local copies, waits for them, and re-layouts  3.43 us (2%)
  between operations  2.43 us (1%)
    pallas_call x1, Pallas kernels, per_device(): pl.pallas_call(functools.partial(kernel, scale, near_count, far_count), o...  154 us
    unnamed x6, local copies, waits for them, and re-layouts  3.43 us

profile of v3, /device:TPU:0, one launch (start us, length us, event | category | flops | bytes accessed | tf_op | source)
XLA Modules:
  0.0 162.4 jit_solution(9520637622541278865)
XLA Ops:
  0.6 154.2 %shard_map.213 = (f32[768,256]{1,0:T(8,128)}, bf16[2,3,4,320,128]{4,3,2,1,0:T(8,128)(2,1)}, bf16[2,64,128]{2,1,0:T(8,128)(2,1)}, f32[1,1]{1,0:T(1,128)}, bf16[2,2,15,256,768]{4,3,2,1,0:T(8,128)(2,1)}) custom-call(bf16[3072,256]{1,0:T(8,128)(2,1)} %latent.1, s32[1,3072]{1,0:T(1,128)} %bitcast.14, s32[5,3072]{1,0:T(8,128)} %actions.1, s32[4,3072]{1,0:T(4,128)} %chances.1, ...), custom_call_target="tpu_custom_call" | custom-call | tf_op jit(solution)/shard_map/pallas_call | solution.py:980
  154.8 0.0 copy-start
  154.9 1.5 copy-done
  156.4 0.0 copy-start.1
  156.4 1.1 copy-done.1
  157.5 0.0 copy-start.2
  157.5 0.8 copy-done.2
  158.3 2.3 %shard_map.214 = (f32[768,1,256]{2,1,0:T(1,128)}, f32[1,2,256,256]{3,2,1,0:T(8,128)}, f32[1,2,2,2,256,256]{5,4,3,2,1,0:T(8,128)}, f32[1,4,256]{2,1,0:T(4,128)}, ...) custom-call(f32[768,256]{1,0:T(8,128)S(1)} %copy-done.1, ...), custom_call_target="tpu_custom_call" | custom-call | tf_op jit(solution)/shard_map/pallas_call | solution.py:1001
Async XLA Ops:
  154.8 1.5 copy-start
  156.4 1.1 copy-start.1
  157.5 0.8 copy-start.2

commit v4 on v3

--- a/solution.py
+++ b/solution.py
@@ -39,11 +39,12 @@
 BAND = 32
 QUARTER = 320
 LAST = 384
-CHAIN = ((0, 1), (1, 2), (2, 3), (3, 4), (4, 6), (6, 8), (8, 10))
-EARLY = (7, 0, 1, 2, 3, 4)
-LATE = (5, 6)
+CHAIN = ((0, 1), (1, 2), (2, 3), (3, 4), (4, 5), (5, 6), (6, 8), (8, 10))
+EARLY = (0, 8, 1, 2, 3, 4)
+LATE = (5, 6, 7)
 MESH = pl.DeviceIdType.MESH
 TICK_AT = 1
+PLACE = (4, 3, 0, 1, 2)
 PART_LAG, NEAR_LAG, FILL_LAG, OWN_LAG, DONE_LAG = 2, 4, 6, 9, 10
 
 
@@ -57,13 +58,14 @@
 
 def kernel(
     scale, near_count, far_count,
-    latent, lengths, actions, chances, values, rewards, entry, blocks, action_w, chance_w, gains, shifts,
-    state_head, chance_head,
-    latent_out, both, misc_both, loss_out, spill,
-    weights, misc, head, acts, inv, ids, onehot, current, resid, prod_a, prod_b, grad, gb, acc_dy, acc_p,
+    latent, lengths_in, actions_in, chances_in, values_in, rewards_in, entry, blocks, action_in, chance_in, gains_in,
+    shifts_in, state_in, chance_head_in,
+    latent_to, both_to, misc_to, loss_out, spill,
+    weights, misc, head, acts, inv, ids, onehot, current, resid, prod_a, prod_b, grad, gb, acc,
     logits, dlogits, dchance, head_back, head_sum, chead_sum, misc_grad, loss_sum, sel, stage, states,
     sent, core_in, core_sum, part_in, part_sum, near_in, far_in, quarter, loss_in,
-    load_sem, spill_sem, chain_send, chain_recv, give_send, step_recv, pass_send, pair_send, pair_recv,
+    lengths, actions, chances, values, rewards, action_w, chance_w, gains, shifts, state_head, chance_head,
+    pick, latent_out, both, misc_both, load_sem, small_sem, out_sem, spill_sem, chain_send, chain_recv, give_send, step_recv, pass_send, pair_send, pair_recv,
     core_send, core_recv, part_send, part_recv, near_send, near_recv, far_send, far_recv,
     fill_send, fill_recv, own_send, own_recv, lane_send, lane_recv, extra_send, extra_recv, loss_send, loss_recv,
 ):
@@ -107,12 +109,116 @@
     loads = [(entry.at[0, 0], weights.at[section, 0]), (blocks.at[0, 0], weights.at[section, 1:5])]
     loads += [(entry.at[0, 1], weights.at[section, 5]), (blocks.at[0, 1], weights.at[section, 6:10])]
     loads += [(latent, states)]
+    small = [(chance_in, chance_w), (action_in, action_w), (gains_in, gains), (shifts_in, shifts)]
+    small += [(lengths_in, lengths), (actions_in, actions), (chances_in, chances), (values_in, values)]
+    small += [(rewards_in, rewards), (state_in, state_head), (chance_head_in, chance_head)]
+    small = [pltpu.make_async_copy(src, dst, small_sem.at[n]) for n, (src, dst) in enumerate(small)]
     loads = [pltpu.make_async_copy(src, dst, load_sem.at[n]) for n, (src, dst) in enumerate(loads)]
-    for load in loads:
+    for load in loads[0:4] + small + loads[4:]:
         load.start()
-    head[head_width // 16 * 16 : head_pad] = jnp.zeros((head_pad - head_width // 16 * 16, feat), BF16)
-    head[0:head_width] = state_head[...]
-
+
+    def send(src, dst, sender, receiver, peer):
+        return pltpu.make_async_remote_copy(
+            src_ref=src, dst_ref=dst, send_sem=sender, recv_sem=receiver, device_id=peer, device_id_type=MESH
+        )
+
+    def landed(dst, receiver):
+        send(dst, dst, load_sem.at[7], receiver, {"dp": mate}).wait_recv()
+
+    place = jnp.where(section >= 2, 5 - section, section)
+    after = lax.rem(place + 1 + 2 * core, steps)
+    after = jnp.where(after >= 2, 5 - after, after)
+    hops = jnp.where(core == 0, place, lax.rem(steps - place, steps))
+    side_a = section + 1 - 2 * lax.rem(section, 2)
+    side_b = lax.rem(section + 2, steps)
+    pass_step = jnp.where(core == 0, side_a, side_b)
+    pass_to = jnp.where(core == 0, side_b, side_a)
+
+    def half_of(step, first, last, part):
+        at = pl.multiple_of(part * (feat // 2), feat // 2)
+        return weights.at[step, first:last, pl.ds(at, feat // 2)]
+
+    def misc_half(step, part):
+        return misc.at[step, pl.ds(pl.multiple_of(part * (MISC_ROWS // 2), MISC_ROWS // 2), MISC_ROWS // 2)]
+
+    def piece(step, n, part):
+        if isinstance(step, int) and step == 0:
+            return misc_half(0, part) if n == len(CHAIN) else half_of(0, *CHAIN[n], part)
+        return misc_half(step, part) if n == 2 else half_of(step, 5 * n, 5 * n + 5, part)
+
+    def chain(n):
+        ref = piece(0, n, core)
+        return send(ref, ref, chain_send.at[n], chain_recv.at[n], {"section": after})
+
+    def give(way, n):
+        ref = piece(section, n, core)
+        return send(ref, ref, give_send.at[way, n], step_recv.at[section, n], {"section": (side_a, side_b)[way]})
+
+    def hand_on(n):
+        ref = piece(pass_step, n, core)
+        return send(ref, ref, pass_send.at[n], step_recv.at[pass_step, n], {"section": pass_to})
+
+    def pair(step, n):
+        ref = piece(step, n, core)
+        return send(ref, ref, pair_send.at[step, n], pair_recv.at[step, n], {"dp": mate})
+
+    def chain_on(order, onward):
+        def run():
+            for n in order:
+                landed(piece(0, n, core), chain_recv.at[n])
+                if onward:
+                    chain(n).start()
+                pair(0, n).start()
+
+        return run
+
+    def need_first(order):
+        def run():
+            for n in order:
+                landed(piece(0, n, 1 - core), pair_recv.at[0, n])
+
+        when(section != 0, run)
+
+    def hand_on_now(condition, pieces):
+        def run():
+            for n in pieces:
+                landed(piece(pass_step, n, core), step_recv.at[pass_step, n])
+                hand_on(n).start()
+
+        when(condition, run)
+
+    def pair_now(step, pieces):
+        def run():
+            for n in pieces:
+                pl.when(pass_step != step)(functools.partial(landed, piece(step, n, core), step_recv.at[step, n]))
+                pair(step, n).start()
+
+        when(section != step, run)
+
+    def need(step, pieces):
+        def run():
+            for n in pieces:
+                landed(piece(step, n, 1 - core), pair_recv.at[step, n])
+
+        when(section != step, run)
+
+    def give_now(way):
+        def run():
+            for n in (2, 0, 1):
+                give(way, n).start()
+
+        return run
+
+    pl.semaphore_wait(barrier, len(peers))
+    for load in loads[0:2]:
+        load.wait()
+
+    @pl.when(hops == 0)
+    def _():
+        chain(0).start()
+
+    for load in small[0:4]:
+        load.wait()
     packed = jnp.concatenate(
         [
             chance_w[0].astype(F32),
@@ -127,105 +233,17 @@
     )
     misc[section] = packed.astype(BF16)
 
-    def send(src, dst, sender, receiver, peer):
-        return pltpu.make_async_remote_copy(
-            src_ref=src, dst_ref=dst, send_sem=sender, recv_sem=receiver, device_id=peer, device_id_type=MESH
-        )
-
-    def landed(dst, receiver):
-        send(dst, dst, load_sem.at[7], receiver, {"dp": mate}).wait_recv()
-
-    place = jnp.where(section >= 2, 5 - section, section)
-    after = lax.rem(place + 1 + 2 * core, steps)
-    after = jnp.where(after >= 2, 5 - after, after)
-    hops = jnp.where(core == 0, place, lax.rem(steps - place, steps))
-    side_a = section + 1 - 2 * lax.rem(section, 2)
-    side_b = lax.rem(section + 2, steps)
-    pass_step = jnp.where(core == 0, side_a, side_b)
-    pass_to = jnp.where(core == 0, side_b, side_a)
-
-    def half_of(step, first, last, part):
-        at = pl.multiple_of(part * (feat // 2), feat // 2)
-        return weights.at[step, first:last, pl.ds(at, feat // 2)]
-
-    def misc_half(step, part):
-        return misc.at[step, pl.ds(pl.multiple_of(part * (MISC_ROWS // 2), MISC_ROWS // 2), MISC_ROWS // 2)]
-
-    def piece(step, n, part):
-        if isinstance(step, int) and step == 0:
-            return misc_half(0, part) if n == 7 else half_of(0, *CHAIN[n], part)
-        return misc_half(step, part) if n == 2 else half_of(step, 5 * n, 5 * n + 5, part)
-
-    def chain(n):
-        ref = piece(0, n, core)
-        return send(ref, ref, chain_send.at[n], chain_recv.at[n], {"section": after})
-
-    def give(way, n):
-        ref = piece(section, n, core)
-        return send(ref, ref, give_send.at[way, n], step_recv.at[section, n], {"section": (side_a, side_b)[way]})
-
-    def hand_on(n):
-        ref = piece(pass_step, n, core)
-        return send(ref, ref, pass_send.at[n], step_recv.at[pass_step, n], {"section": pass_to})
-
-    def pair(step, n):
-        ref = piece(step, n, core)
-        return send(ref, ref, pair_send.at[step, n], pair_recv.at[step, n], {"dp": mate})
-
-    def chain_on(order, onward):
-        def run():
-            for n in order:
-                landed(piece(0, n, core), chain_recv.at[n])
-                if onward:
-                    chain(n).start()
-                pair(0, n).start()
-
-        return run
-
-    def need_first(order):
-        def run():
-            for n in order:
-                landed(piece(0, n, 1 - core), pair_recv.at[0, n])
-
-        when(section != 0, run)
-
-    def hand_on_now(condition, pieces):
-        def run():
-            for n in pieces:
-                landed(piece(pass_step, n, core), step_recv.at[pass_step, n])
-                hand_on(n).start()
-
-        when(condition, run)
-
-    def pair_now(step, pieces):
-        def run():
-            for n in pieces:
-                pl.when(pass_step != step)(functools.partial(landed, piece(step, n, core), step_recv.at[step, n]))
-                pair(step, n).start()
-
-        when(section != step, run)
-
-    def need(step, pieces):
-        def run():
-            for n in pieces:
-                landed(piece(step, n, 1 - core), pair_recv.at[step, n])
-
-        when(section != step, run)
-
-    def give_now(way):
-        def run():
-            for n in (2, 0, 1):
-                give(way, n).start()
-
-        return run
-
-    pl.semaphore_wait(barrier, len(peers))
-    for load in loads[0:4]:
-        load.wait()
-
     @pl.when(hops == 0)
     def _():
-        for n in EARLY + LATE:
+        for n in EARLY[1:]:
+            chain(n).start()
+
+    for load in loads[2:4]:
+        load.wait()
+
+    @pl.when(hops == 0)
+    def _():
+        for n in LATE:
             chain(n).start()
 
     pl.when(section == 1)(give_now(0))
@@ -233,6 +251,16 @@
 
     pick_at = lax.broadcasted_iota(jnp.int32, (steps * WIDE, WIDE), 0)
     pick_to = lax.broadcasted_iota(jnp.int32, (steps * WIDE, WIDE), 1)
+    for tower in range(2):
+        row = lax.broadcasted_iota(jnp.int32, (MISC_ROWS, 2 * NORMS * LANES), 0)
+        at = lax.broadcasted_iota(jnp.int32, (MISC_ROWS, 2 * NORMS * LANES), 1) // LANES
+        chosen = jnp.where((at < NORMS) & (row == GAIN_ROW + tower * NORMS + at), 8.0, 0.0)
+        chosen = chosen + jnp.where((at >= NORMS) & (row == SHIFT_ROW + tower * NORMS + at - NORMS), 0.5, 0.0)
+        pick[tower] = chosen.astype(BF16)
+    for load in small[4:]:
+        load.wait()
+    head[head_width // 16 * 16 : head_pad] = jnp.zeros((head_pad - head_width // 16 * 16, feat), BF16)
+    head[0:head_width] = state_head[...]
     sel[...] = (pick_at == steps * pick_to + section).astype(F32).astype(BF16)
     stage[...] = jnp.zeros_like(stage)
     stage[0:1] = lengths[...].astype(F32)
@@ -270,14 +298,8 @@
     need_first(EARLY)
 
     def spread_norms(k, tower, with_shift):
-        count = 2 * NORMS if with_shift else NORMS
-        row = lax.broadcasted_iota(jnp.int32, (MISC_ROWS, count * LANES), 0)
-        at = lax.broadcasted_iota(jnp.int32, (MISC_ROWS, count * LANES), 1) // LANES
-        gain_row = GAIN_ROW + tower * NORMS
-        shift_row = SHIFT_ROW + tower * NORMS
-        pick = jnp.where((at < NORMS) & (row == gain_row + at), 8.0, 0.0)
-        pick = pick + jnp.where((at >= NORMS) & (row == shift_row + at - NORMS), 0.5, 0.0)
-        gb[:, 0 : count * LANES] = contract(misc[k], pick.astype(BF16), 0, 0)
+        width = (2 * NORMS if with_shift else NORMS) * LANES
+        gb[:, 0:width] = contract(misc[k], pick[tower, :, 0:width], 0, 0)
 
     def gain_of(n, band=slice(None)):
         return gb[band, n * LANES : (n + 1) * LANES]
@@ -330,30 +352,41 @@
                     apply(n, sub, values[:, c * LANES : (c + 1) * LANES])
 
     def softmax_block(pieces, target, live):
+        bands = []
+        for start, stop, low, high in pieces:
+            for at in range(start, stop, BAND):
+                bands.append((at, min(at + BAND, stop), low, high, (low, high) != (start, stop)))
+
+        def fold(values, op):
+            parts = [values[r : r + 8] for r in range(0, values.shape[0], 8)]
+            return functools.reduce(op, parts)
+
         top = None
-        for start, stop, low, high in pieces:
+        for start, stop, low, high, mixed in bands:
             part = logits[start:stop]
-            if (low, high) != (start, stop):
+            if mixed:
                 row = lax.broadcasted_iota(jnp.int32, part.shape, 0) + start
                 part = jnp.where((row >= low) & (row < high), part, -jnp.inf)
-            best = jnp.max(part, axis=0, keepdims=True)
+            best = fold(part, jnp.maximum)
             top = best if top is None else jnp.maximum(top, best)
-        total = None
-        hit = None
-        for start, stop, low, high in pieces:
+        top = jnp.max(top, axis=0, keepdims=True)
+        total, hit = None, None
+        for start, stop, low, high, mixed in bands:
             part = logits[start:stop] - top
-            row = lax.broadcasted_iota(jnp.int32, part.shape, 0) + start
-            found = jnp.sum(jnp.where(row == target, part, 0.0), axis=0, keepdims=True)
+            row = lax.broadcasted_iota(jnp.int32, part.shape, 0)
+            found = fold(jnp.where(row == target - start, part, 0.0), jnp.add)
             expo = jnp.exp(part)
-            if (low, high) != (start, stop):
-                keep = (row >= low) & (row < high)
+            if mixed:
+                keep = (row >= low - start) & (row < high - start)
                 expo = jnp.where(keep, expo, 0.0)
                 logits[start:stop] = jnp.where(keep, expo, logits[start:stop])
             else:
                 logits[start:stop] = expo
-            amount = jnp.sum(expo, axis=0, keepdims=True)
+            amount = fold(expo, jnp.add)
             total = amount if total is None else total + amount
             hit = found if hit is None else hit + found
+        total = jnp.sum(total, axis=0, keepdims=True)
+        hit = jnp.sum(hit, axis=0, keepdims=True)
         return live * (jnp.log(total) - hit), live / total
 
     def head_pass(k, tick):
@@ -389,19 +422,16 @@
                     scales.append(scale)
                 low_a = bins // 16 * 16
                 low_b = 2 * bins // 16 * 16
-                for start, stop in (
-                    (0, low_a),
-                    (low_a, low_a + 16),
-                    (low_a + 16, low_b),
-                    (low_b, low_b + 16),
-                ):
-                    row = lax.broadcasted_iota(jnp.int32, (stop - start, LANES), 0) + start
+                cuts = [*range(0, low_a, BAND), low_a, *range(low_a + 16, low_b, BAND), low_b, low_b + 16]
+                for start, stop in zip(cuts[:-1], cuts[1:]):
+                    row = lax.broadcasted_iota(jnp.int32, (stop - start, LANES), 0)
                     expo = logits[start:stop]
                     if stop <= bins:
-                        delta = expo * scales[0] - jnp.where(row == value_at, live, 0.0)
+                        delta = expo * scales[0] - jnp.where(row == value_at - start, live, 0.0)
                     elif start >= bins and stop <= 2 * bins:
-                        delta = expo * scales[1] - jnp.where(row == reward_at, live, 0.0)
+                        delta = expo * scales[1] - jnp.where(row == reward_at - start, live, 0.0)
                     else:
+                        row = row + start
                         scale = jnp.where(row < bins, scales[0], jnp.where(row < 2 * bins, scales[1], scales[2]))
                         delta = expo * scale
                         for target in (value_at, reward_at, policy_at):
@@ -541,182 +571,174 @@
     def lanes(part):
         return pl.ds(pl.multiple_of(part * LANES, LANES), LANES)
 
-    def core_copy(b, slot, count):
+    def span(b):
+        if isinstance(b, int) and b >= batches:
+            return (b - batches) * (LAST // 2), LAST // 2
+        return 0, QUARTER
+
+    def held(b):
+        return min(b, batches) if isinstance(b, int) else b
+
+    def rows_of(b):
+        low, count = span(b)
+        return slice(low, low + count)
+
+    def matrix_rows(b):
+        low, count = span(b)
+        return slice(low, min(low + count, QUARTER))
+
+    def turn(b, tower):
+        return 3 if isinstance(b, int) and b > batches else tower
+
+    def core_copy(b, slot):
         return send(
-            sent.at[slot, :, 0:count, lanes(1 - core)], core_in.at[slot, :, 0:count],
+            sent.at[slot, :, rows_of(b), lanes(1 - core)], core_in.at[slot, :, rows_of(b)],
             core_send.at[b], core_recv.at[b], {"dp": mate},
         )
 
-    def part_copy(b, slot, count, offset):
+    def part_copy(b, slot, offset):
         return send(
-            core_sum.at[slot, section_at(offset), 0:count], part_in.at[b, offset - 1, 0:count],
+            core_sum.at[slot, section_at(offset), rows_of(b)], part_in.at[b, offset - 1, 0 : span(b)[1]],
             part_send.at[b, offset - 1], part_recv.at[b, offset - 1], {"section": section_at(offset)},
         )
 
-    def near_rows(count, offset):
+    def near_rows(b, offset):
+        low, count = span(b)
         size = count // near_count
-        return pl.ds(pl.multiple_of(lax.rem(near + offset, near_count) * size, 16), size)
-
-    def near_copy(b, slot, count, offset):
+        return pl.ds(pl.multiple_of(low + lax.rem(near + offset, near_count) * size, 16), size)
+
+    def near_copy(b, slot, offset):
         return send(
-            part_sum.at[slot, near_rows(count, offset)], near_in.at[b, offset - 1, 0 : count // near_count],
+            part_sum.at[slot, near_rows(b, offset)], near_in.at[b, offset - 1, 0 : span(b)[1] // near_count],
             near_send.at[b, offset - 1], near_recv.at[b, offset - 1], {"dp": near_line(offset)},
         )
 
-    def far_copy(b, slot, count, offset):
+    def far_copy(b, offset):
         return send(
-            quarter.at[b, near_rows(count, 0)], far_in.at[b, offset - 1, 0 : count // near_count],
+            quarter.at[held(b), near_rows(b, 0)], far_in.at[b, offset - 1, 0 : span(b)[1] // near_count],
             far_send.at[b, offset - 1], far_recv.at[b, offset - 1], {"dp": far_line(offset)},
         )
 
-    def fill_back(b, count, offset):
-        ref = quarter.at[b, near_rows(count, 0)]
+    def fill_back(b, offset):
+        ref = quarter.at[held(b), near_rows(b, 0)]
         return send(ref, ref, fill_send.at[b, offset - 1], fill_recv.at[b, offset - 1], {"dp": near_line(offset)})
 
-    def core_wait(b, slot, count):
-        core_copy(b, slot, count).wait()
+    def core_wait(b, slot):
+        core_copy(b, slot).wait()
         for j in range(steps):
-            mine = sent[slot, j, 0:count, lanes(core)].astype(F32)
-            core_sum[slot, j, 0:count] = (mine + core_in[slot, j, 0:count].astype(F32)).astype(BF16)
+            mine = sent[slot, j, rows_of(b), lanes(core)].astype(F32)
+            core_sum[slot, j, rows_of(b)] = (mine + core_in[slot, j, rows_of(b)].astype(F32)).astype(BF16)
         for offset in range(1, steps):
-            part_copy(b, slot, count, offset).start()
-
-    def part_wait(b, slot, count):
+            part_copy(b, slot, offset).start()
+
+    def part_wait(b, slot):
         for offset in range(1, steps):
-            part_copy(b, slot, count, offset).wait()
-        total = core_sum[slot, section, 0:count].astype(F32)
+            part_copy(b, slot, offset).wait()
+        total = core_sum[slot, section, rows_of(b)].astype(F32)
         for n in range(steps - 1):
-            total = total + part_in[b, n, 0:count].astype(F32)
-        part_sum[slot, 0:count] = total.astype(BF16)
+            total = total + part_in[b, n, 0 : span(b)[1]].astype(F32)
+        part_sum[slot, rows_of(b)] = total.astype(BF16)
         for offset in range(1, near_count):
-            near_copy(b, slot, count, offset).start()
-
-    def near_wait(b, slot, count):
+            near_copy(b, slot, offset).start()
+
+    def near_wait(b, slot):
         for offset in range(1, near_count):
-            near_copy(b, slot, count, offset).wait()
-        size = count // near_count
-        total = part_sum[slot, near_rows(count, 0)].astype(F32)
+            near_copy(b, slot, offset).wait()
+        size = span(b)[1] // near_count
+        total = part_sum[slot, near_rows(b, 0)].astype(F32)
         for n in range(near_count - 1):
             total = total + near_in[b, n, 0:size].astype(F32)
-        quarter[b, near_rows(count, 0)] = total.astype(BF16)
+        quarter[held(b), near_rows(b, 0)] = total.astype(BF16)
         if far_count > 1:
             for offset in range(1, far_count):
-                far_copy(b, slot, count, offset).start()
+                far_copy(b, offset).start()
             for offset in range(1, far_count):
-                far_copy(b, slot, count, offset).wait()
+                far_copy(b, offset).wait()
             for n in range(far_count - 1):
                 total = total + far_in[b, n, 0:size].astype(F32)
-            quarter[b, near_rows(count, 0)] = total.astype(BF16)
+            quarter[held(b), near_rows(b, 0)] = total.astype(BF16)
         for offset in range(1, near_count):
-            fill_back(b, count, offset).start()
-
-    def fill_wait(b, count):
+            fill_back(b, offset).start()
+
+    def fill_wait(b):
         for offset in range(1, near_count):
-            fill_back(b, count, offset).wait_send()
-            landed(quarter.at[b, near_rows(count, near_count - offset)], fill_recv.at[b, offset - 1])
+            fill_back(b, offset).wait_send()
+            landed(quarter.at[held(b), near_rows(b, near_count - offset)], fill_recv.at[b, offset - 1])
 
     def owner_copy(b, tower, offset):
         return send(
-            quarter.at[b, 0:QUARTER], both.at[core, tower, section], own_send.at[b, offset - 1],
-            own_recv.at[tower, offset - 1], {"section": section_at(steps - offset)},
+            quarter.at[held(b), matrix_rows(b)], both.at[core, tower, section, matrix_rows(b)],
+            own_send.at[b, offset - 1], own_recv.at[turn(b, tower), offset - 1], {"section": section_at(steps - offset)},
         )
+
+    def owner_of(b):
+        return 0 if isinstance(b, int) and b >= batches else steps - 1 - (b - 1) // 2
 
     def share_start(b, tower):
         def keep():
-            both[core, tower, section] = quarter[b, 0:QUARTER]
+            both[core, tower, section, matrix_rows(b)] = quarter[held(b), matrix_rows(b)]
 
         if tower == 2:
             keep()
             for offset in range(1, steps):
                 owner_copy(b, tower, offset).start()
             return
-        owner = steps - 1 - (b - 1) // 2
-        pl.when(section == owner)(keep)
+        pl.when(section == owner_of(b))(keep)
         for offset in range(1, steps):
-            pl.when(lax.rem(section - owner + steps, steps) == offset)(owner_copy(b, tower, offset).start)
+            pl.when(lax.rem(section - owner_of(b) + steps, steps) == offset)(owner_copy(b, tower, offset).start)
 
     def share_wait(b, tower):
         def take():
             for offset in range(1, steps):
-                landed(both.at[core, tower, section_at(offset)], own_recv.at[tower, offset - 1])
-            lane_copy(tower).start()
+                landed(
+                    both.at[core, tower, section_at(offset), matrix_rows(b)], own_recv.at[turn(b, tower), offset - 1]
+                )
+            lane_copy(b, tower).start()
 
         if tower == 2:
             for offset in range(1, steps):
                 owner_copy(b, tower, offset).wait_send()
             take()
             return
-        owner = steps - 1 - (b - 1) // 2
         for offset in range(1, steps):
-            pl.when(lax.rem(section - owner + steps, steps) == offset)(owner_copy(b, tower, offset).wait_send)
-        pl.when(section == owner)(take)
-
-    def lane_copy(tower):
-        ref = both.at[core, tower]
-        return send(ref, ref, lane_send.at[tower], lane_recv.at[tower], {"dp": mate})
+            pl.when(lax.rem(section - owner_of(b) + steps, steps) == offset)(owner_copy(b, tower, offset).wait_send)
+        pl.when(section == owner_of(b))(take)
+
+    def lane_copy(b, tower):
+        ref = both.at[core, tower, :, matrix_rows(b)]
+        return send(ref, ref, lane_send.at[turn(b, tower)], lane_recv.at[turn(b, tower)], {"dp": mate})
 
     def finish(b, tower):
         def run():
-            lane_copy(tower).wait_send()
-            landed(both.at[1 - core, tower], lane_recv.at[tower])
+            lane_copy(b, tower).wait_send()
+            landed(both.at[1 - core, tower, :, matrix_rows(b)], lane_recv.at[turn(b, tower)])
 
         if tower == 2:
             run()
         else:
-            pl.when(section == steps - 1 - (b - 1) // 2)(run)
+            pl.when(section == owner_of(b))(run)
 
     def by_kind(b, odd, action):
-        if isinstance(b, int):
-            if 0 <= b <= batches:
-                action(b, 1 if odd else (2 if b == 0 else 0))
-        elif odd:
+        if odd:
             pl.when(b >= 0)(functools.partial(action, b, 1))
         else:
             pl.when(b > 0)(functools.partial(action, b, 0))
             pl.when(b == 0)(functools.partial(action, b, 2))
 
-    def rows_of(b):
-        return LAST if isinstance(b, int) and b == batches else QUARTER
-
     def fill_and_share(b, tower):
-        fill_wait(b, rows_of(b))
+        fill_wait(b)
         share_start(b, tower)
 
     def ticks(at, parity):
-        inside = not isinstance(at, int)
-
         def odd(lag):
             return (parity + lag) % 2 == 1
 
         by_kind(at - DONE_LAG, odd(DONE_LAG), finish)
         by_kind(at - OWN_LAG, odd(OWN_LAG), share_wait)
         by_kind(at - FILL_LAG, odd(FILL_LAG), fill_and_share)
-        if inside:
-            pl.when(at >= NEAR_LAG)(functools.partial(near_wait, at - NEAR_LAG, parity, QUARTER))
-            pl.when(at >= PART_LAG)(functools.partial(part_wait, at - PART_LAG, parity, QUARTER))
-            core_wait(at, parity, QUARTER)
-        else:
-            if at - NEAR_LAG <= batches:
-                near_wait(at - NEAR_LAG, parity, rows_of(at - NEAR_LAG))
-            if at - PART_LAG <= batches:
-                part_wait(at - PART_LAG, parity, rows_of(at - PART_LAG))
-            if at <= batches:
-                core_wait(at, parity, rows_of(at))
-
-    def norm_backward(d_out, slope, unit, gain, inverse, at, first):
-        d_two = d_out * slope.astype(F32)
-        unit = unit.astype(F32)
-        weighted = d_two * unit
-        if first:
-            acc_dy[at] = d_two
-            acc_p[at] = weighted
-        else:
-            acc_dy[at] += d_two
-            acc_p[at] += weighted
-        d_unit = d_two * gain
-        mean = jnp.sum(d_unit, axis=0, keepdims=True) * (1.0 / WIDE)
-        along = jnp.sum(weighted * gain, axis=0, keepdims=True)
-        return ((d_unit - mean - unit * along) * inverse).astype(BF16), d_two
+        pl.when(at >= NEAR_LAG)(functools.partial(near_wait, at - NEAR_LAG, parity))
+        pl.when(at >= PART_LAG)(functools.partial(part_wait, at - PART_LAG, parity))
+        core_wait(at, parity)
 
     def tower_backward(k, tower, at):
         slot = lax.rem(k, 2)
@@ -726,44 +748,61 @@
 
         def put(m, value):
             size = feat // steps
+            at_row = PLACE[m] * size
             for j in range(steps):
-                sent[slot_out, j, m * size : (m + 1) * size] = value[j * size : (j + 1) * size].astype(BF16)
-
-
-        def norm_of(d_out, at, sub):
-            return norm_backward(
-                d_out,
-                act[10 + at, :, sub],
-                act[5 + at, :, sub],
-                gain_of(at),
-                inv[2 * k + tower, at : at + 1, sub],
-                at,
-                sub.start == 0,
-            )
+                sent[slot_out, j, at_row : at_row + size] = value[j * size : (j + 1) * size].astype(BF16)
+
+        def norm_of(d_out, at, sub, target, keep):
+            means, along = None, None
+            kept = []
+            for r in range(0, feat, BAND):
+                band = slice(r, r + BAND)
+                d_two = d_out[band] * act[10 + at, band, sub].astype(F32)
+                weighted = d_two * act[5 + at, band, sub].astype(F32)
+                if sub.start == 0:
+                    acc[NORMS + at, band] = d_two
+                    acc[at, band] = weighted
+                else:
+                    acc[NORMS + at, band] += d_two
+                    acc[at, band] += weighted
+                if keep:
+                    grad[band, sub] = 0.5 * d_two
+                gain = gain_of(at, band)
+                d_unit = d_two * gain
+                kept.append(d_unit)
+                part_mean = jnp.sum(d_unit.reshape(BAND // 8, 8, LANES), axis=0)
+                part_along = jnp.sum((weighted * gain).reshape(BAND // 8, 8, LANES), axis=0)
+                means = part_mean if means is None else means + part_mean
+                along = part_along if along is None else along + part_along
+            mean = jnp.sum(means, axis=0, keepdims=True) * (1.0 / feat)
+            along = jnp.sum(along, axis=0, keepdims=True)
+            inverse = inv[2 * k + tower, at : at + 1, sub]
+            for n, r in enumerate(range(0, feat, BAND)):
+                band = slice(r, r + BAND)
+                unit = act[5 + at, band, sub].astype(F32)
+                target[band, sub] = ((kept[n] - mean - unit * along) * inverse).astype(BF16)
 
         for j in (1, 0):
             outer = 2 + 2 * j
             inner = 1 + 2 * j
             for part in chunks:
                 for sub in subs(part):
-                    d_post, d_two = norm_of(grad[:, sub], outer, sub)
-                    prod_a[:, sub] = d_post
-                    grad[:, sub] = 0.5 * d_two
+                    norm_of(grad[:, sub], outer, sub, prod_a, True)
             if j == TICK_AT:
                 ticks(at, 1 - tower)
             for part in chunks:
                 d_mid = contract(weights[k, 5 * tower + 2 + 2 * j], prod_a[:, part], 1, 0)
                 for n, sub in enumerate(subs(part)):
-                    d_pre, _ = norm_of(d_mid[:, n * LANES : (n + 1) * LANES], inner, sub)
-                    prod_b[:, sub] = d_pre
+                    norm_of(d_mid[:, n * LANES : (n + 1) * LANES], inner, sub, prod_b, False)
             put(2 + 2 * j, contract(act[3 + j], prod_a[...], 1, 1))
+            if tower == 0 and j == 0:
+                pl.when(k == 0)(core_copy(batches, 0).start)
             for part in chunks:
                 grad[:, part] += contract(weights[k, 5 * tower + 1 + 2 * j], prod_b[:, part], 1, 0)
             put(1 + 2 * j, contract(act[1 + j], prod_b[...], 1, 1))
         for part in chunks:
             for sub in subs(part):
-                d_first, _ = norm_of(grad[:, sub], 0, sub)
-                prod_a[:, sub] = d_first
+                norm_of(grad[:, sub], 0, sub, prod_a, False)
         look = lookup(k, tower)
         put(0, contract(act[0], prod_a[...], 1, 1))
         got = contract(onehot[look], prod_a[...], 1, 1)
@@ -772,16 +811,18 @@
         else:
             misc_grad[k, 0:32] = got
         ones = jnp.ones((16, LANES), BF16)
+        both_sums = acc[...].reshape(2 * NORMS * feat, LANES).astype(BF16)
+        total = contract(ones, both_sums, 1, 1)
         for n in range(NORMS):
-            total = contract(ones, acc_p[n].astype(BF16), 1, 1)
-            misc_grad[k, GAIN_ROW + NORMS * tower + n : GAIN_ROW + NORMS * tower + n + 1] = 8.0 * total[0:1]
-            total = contract(ones, acc_dy[n].astype(BF16), 1, 1)
-            misc_grad[k, SHIFT_ROW + NORMS * tower + n : SHIFT_ROW + NORMS * tower + n + 1] = 0.5 * total[0:1]
+            at_gain = GAIN_ROW + NORMS * tower + n
+            at_shift = SHIFT_ROW + NORMS * tower + n
+            misc_grad[k, at_gain : at_gain + 1] = 8.0 * total[0:1, n * feat : (n + 1) * feat]
+            misc_grad[k, at_shift : at_shift + 1] = 0.5 * total[0:1, (NORMS + n) * feat : (NORMS + n + 1) * feat]
 
     head_sum[head_width : head_width + chance_count] = chead_sum[...]
     for j in range(steps):
         sent[0, j, 0:QUARTER] = head_sum[j * QUARTER : (j + 1) * QUARTER].astype(BF16)
-    core_copy(0, 0, QUARTER).start()
+    core_copy(0, 0).start()
 
     @pl.loop(0, steps)
     def _(back):
@@ -802,7 +843,7 @@
             grad[...] = (0.5 * grad[...]).astype(BF16).astype(F32) + head_back[k]
 
         tower_backward(k, 1, 2 * back)
-        core_copy(2 * back + 1, 1, QUARTER).start()
+        core_copy(2 * back + 1, 1).start()
         for part in chunks:
             grad[:, part] = contract(weights[k, 5], prod_a[:, part], 1, 0) + contract(
                 chance_head[...], dchance[k, :, part], 0, 0
@@ -811,25 +852,20 @@
 
         @pl.when(k > 0)
         def _():
-            core_copy(2 * back + 2, 0, QUARTER).start()
+            core_copy(2 * back + 2, 0).start()
 
         @pl.when(k > 0)
         def _():
             for part in chunks:
                 grad[:, part] = contract(weights[k, 0], prod_a[:, part], 1, 0)
 
-        @pl.when(k == 0)
-        def _():
-            for part in chunks:
-                latent_out[part] = 0.5 * contract(prod_a[:, part], weights[0, 0], 0, 1)
-
         @pl.when(k >= 2)
         def _():
             fill_copy(k - 2).start()
 
     for j in range(steps):
         sent[0, j, QUARTER:LAST] = misc_grad[j].astype(BF16)
-    core_copy(batches, 0, LAST).start()
+    core_copy(batches + 1, 0).start()
 
     loss_at = [{"dp": mate}] + [{"section": section_at(o)} for o in range(1, steps)]
     loss_at += [{"dp": near_line(o)} for o in range(1, near_count)]
@@ -857,39 +893,93 @@
         )
 
     loss_start(0)
-    for at in range(batches, batches + DONE_LAG + 1):
-        ticks(at, at % 2)
-        if at < batches + 3:
-            loss_wait(at - batches)
-            loss_start(at - batches + 1)
-        if at == batches + FILL_LAG:
-            misc_copy().start()
+    def run(phase, *numbers):
+        for b in numbers:
+            if phase is finish or phase is share_wait or phase is fill_and_share:
+                phase(b, 2 if b == 0 else (0 if b > batches else b % 2))
+            else:
+                phase(b, 0 if b > batches else b % 2)
+
+    last = batches
+    run(near_wait, last - 4)
+    run(part_wait, last - 2)
+    run(core_wait, last)
+    for part in chunks:
+        latent_out[part] = 0.5 * contract(prod_a[:, part], weights[0, 0], 0, 1)
+    run(core_wait, last + 1)
+    outs = [(latent_out, latent_to), (misc_both, misc_to)]
+    outs += [(both.at[:, n], both_to.at[:, n]) for n in (2, 1, 0)]
+    outs = [pltpu.make_async_copy(src, dst, out_sem.at[n]) for n, (src, dst) in enumerate(outs)]
+    outs[0].start()
+    loss_wait(0)
+    loss_start(1)
+    run(near_wait, last - 3)
+    run(fill_and_share, last - 6, last - 5)
+    run(share_wait, last - 8)
+    run(part_wait, last - 1)
+    run(near_wait, last - 2)
+    run(fill_and_share, last - 4)
+    run(share_wait, last - 7)
+    run(finish, last - 8)
+    run(part_wait, last, last + 1)
+    loss_wait(1)
+    loss_start(2)
+    run(fill_and_share, last - 3)
+    run(near_wait, last - 1)
+    run(fill_and_share, last - 2)
+    run(share_wait, last - 6, last - 5)
+    run(near_wait, last, last + 1)
+    loss_wait(2)
+    loss_start(3)
+    run(fill_and_share, last - 1)
+    run(share_wait, last - 4, last - 3)
+    run(finish, last - 7, last - 6, last - 5)
+    run(fill_and_share, last, last + 1)
+    misc_copy().start()
+    run(share_wait, last - 2, last - 1)
+    run(finish, last - 4, last - 3, last - 2)
+    outs[2].start()
+    run(share_wait, last, last + 1)
+    run(finish, last - 1)
+    outs[3].start()
+    run(finish, last, last + 1)
+    outs[4].start()
     loss_wait(3)
     loss_out[...] = jnp.sum(loss_sum[4, 0:1], axis=1, keepdims=True) * scale
     misc_both[core] = quarter[batches, QUARTER:LAST]
     misc_copy().wait_send()
     landed(misc_both.at[1 - core], extra_recv.at[0])
+    outs[1].start()
+    for out in outs:
+        out.wait()
 
 
 def finish_kernel(
-    scale, latent_in, both, misc_both,
+    scale, latent_from, both_from, misc_from,
     latent_out, entry_out, block_out, action_out, chance_out, gain_out, shift_out, head_out, chead_out,
+    latent_in, both, misc_both, sem,
 ):
+    copies = [(both_from, both), (misc_from, misc_both), (latent_from, latent_in)]
+    copies = [pltpu.make_async_copy(src, dst, sem.at[n]) for n, (src, dst) in enumerate(copies)]
+    for copy in copies:
+        copy.start()
     steps = both.shape[2]
     feat = entry_out.shape[-1]
     size = feat // steps
     head_width = head_out.shape[0]
     chance_count = chead_out.shape[0]
-    latent_out[:, 0, :] = latent_in[...]
+    copies[0].wait()
+    copies[1].wait()
     for part in range(2):
         lanes = slice(part * LANES, (part + 1) * LANES)
         for j in range(steps):
             at = slice(j * size, (j + 1) * size)
             for tower in range(2):
                 got = both[part, tower, j].astype(F32) * scale
-                entry_out[0, tower, at, lanes] = got[0:size]
+                entry_out[0, tower, at, lanes] = got[PLACE[0] * size : (PLACE[0] + 1) * size]
                 for m in range(4):
-                    block_out[0, tower, m // 2, m % 2, at, lanes] = got[(m + 1) * size : (m + 2) * size]
+                    row = PLACE[m + 1] * size
+                    block_out[0, tower, m // 2, m % 2, at, lanes] = got[row : row + size]
             got = both[part, 2, j].astype(F32) * scale
             start = j * QUARTER
             stop = min(start + QUARTER, head_width)
@@ -905,6 +995,8 @@
                 gain_out[0, n, tower : tower + 1, lanes] = got[at : at + 1]
                 at = SHIFT_ROW + tower * NORMS + n
                 shift_out[0, n, tower : tower + 1, lanes] = got[at : at + 1]
+    copies[2].wait()
+    latent_out[:, 0, :] = latent_in[...]
 
 
 def per_device(
@@ -919,7 +1011,7 @@
     feat = latent.shape[1]
     head_width = state_head.shape[1]
     head_pad = steps * QUARTER
-    batches = 2 * steps + 1
+    batches = 2 * steps + 2
     vmem = pl.BlockSpec(memory_space=pltpu.VMEM)
     anys = pl.BlockSpec(memory_space=pl.ANY)
     dma = pltpu.SemaphoreType.DMA
@@ -939,8 +1031,7 @@
         pltpu.VMEM((feat, rows), BF16),
         pltpu.VMEM((feat, rows), F32),
         pltpu.VMEM((feat, 2 * NORMS * LANES), F32),
-        pltpu.VMEM((NORMS, feat, LANES), F32),
-        pltpu.VMEM((NORMS, feat, LANES), F32),
+        pltpu.VMEM((2 * NORMS, feat, LANES), F32),
         pltpu.VMEM((head_pad, LANES), F32),
         pltpu.VMEM((head_pad, rows), BF16),
         pltpu.VMEM((steps, 32, rows), BF16),
@@ -955,24 +1046,41 @@
         pltpu.VMEM((2, steps, LAST, feat), BF16),
         pltpu.VMEM((2, steps, LAST, LANES), BF16),
         pltpu.VMEM((2, steps, LAST, LANES), BF16),
-        pltpu.VMEM((batches, steps - 1, LAST, LANES), BF16),
+        pltpu.VMEM((batches, steps - 1, QUARTER, LANES), BF16),
         pltpu.VMEM((2, LAST, LANES), BF16),
-        pltpu.VMEM((batches, near_count - 1, LAST // near_count, LANES), BF16),
-        pltpu.VMEM((batches, far_slots, LAST // near_count, LANES), BF16),
-        pltpu.VMEM((batches, LAST, LANES), BF16),
+        pltpu.VMEM((batches, near_count - 1, QUARTER // near_count, LANES), BF16),
+        pltpu.VMEM((batches, far_slots, QUARTER // near_count, LANES), BF16),
+        pltpu.VMEM((batches - 1, LAST, LANES), BF16),
         pltpu.VMEM((tiny, 8, LANES), F32),
+        pltpu.VMEM((1, latent.shape[0]), jnp.int32),
+        pltpu.VMEM(actions.shape, jnp.int32),
+        pltpu.VMEM(chances.shape, jnp.int32),
+        pltpu.VMEM(value_bins.shape, jnp.int32),
+        pltpu.VMEM(reward_bins.shape, jnp.int32),
+        pltpu.VMEM(action_w.shape, BF16),
+        pltpu.VMEM(chance_w.shape, BF16),
+        pltpu.VMEM((1, gain_w.shape[2], gain_w.shape[1], feat), BF16),
+        pltpu.VMEM((1, gain_w.shape[2], gain_w.shape[1], feat), BF16),
+        pltpu.VMEM((head_width, feat), BF16),
+        pltpu.VMEM((chance_head.shape[1], feat), BF16),
+        pltpu.VMEM((2, MISC_ROWS, 2 * NORMS * LANES), BF16),
+        pltpu.VMEM((rows, feat), F32),
+        pltpu.VMEM((2, 3, steps, QUARTER, LANES), BF16),
+        pltpu.VMEM((2, MISC_ROWS, LANES), BF16),
         dma((8,)),
+        dma((11,)),
+        dma((6,)),
         dma((4,)),
-        dma((8,)), dma((8,)),
+        dma((9,)), dma((9,)),
         dma((2, 3)), dma((steps, 3)), dma((3,)),
-        dma((steps, 8)), dma((steps, 8)),
+        dma((steps, 9)), dma((steps, 9)),
         dma((batches,)), dma((batches,)),
         dma((batches, steps - 1)), dma((batches, steps - 1)),
         dma((batches, near_count - 1)), dma((batches, near_count - 1)),
         dma((batches, far_slots)), dma((batches, far_slots)),
         dma((batches, near_count - 1)), dma((batches, near_count - 1)),
-        dma((batches, steps - 1)), dma((3, steps - 1)),
-        dma((3,)), dma((3,)),
+        dma((batches, steps - 1)), dma((4, steps - 1)),
+        dma((4,)), dma((4,)),
         dma((1,)), dma((1,)),
         dma((tiny,)), dma((tiny,)),
     ]
@@ -986,8 +1094,8 @@
             jax.ShapeDtypeStruct((1, 1), F32),
             jax.ShapeDtypeStruct((steps - 2, 2, 15, feat, rows), BF16),
         ),
-        in_specs=[anys] + [vmem] * 5 + [anys] * 2 + [vmem] * 6,
-        out_specs=(vmem,) * 4 + (anys,),
+        in_specs=[anys] * 14,
+        out_specs=(anys,) * 3 + (vmem, anys),
         scratch_shapes=scratch,
         compiler_params=pltpu.CompilerParams(
             vmem_limit_bytes=63 * 2**20, collective_id=0, has_side_effects=True
@@ -1011,9 +1119,15 @@
             jax.ShapeDtypeStruct((head_width, feat), F32),
             jax.ShapeDtypeStruct((chance_head.shape[1], feat), F32),
         ),
-        in_specs=[vmem] * 3,
+        in_specs=[anys] * 3,
         out_specs=(vmem,) * 9,
-        compiler_params=pltpu.CompilerParams(vmem_limit_bytes=32 * 2**20),
+        scratch_shapes=[
+            pltpu.VMEM((rows, feat), F32),
+            pltpu.VMEM((2, 3, steps, QUARTER, LANES), BF16),
+            pltpu.VMEM((2, MISC_ROWS, LANES), BF16),
+            dma((3,)),
+        ],
+        compiler_params=pltpu.CompilerParams(vmem_limit_bytes=63 * 2**20),
     )(outs[0], outs[1], outs[2])
     latent_grad, entry_grad, block_grad, action_grad, chance_grad, gain_grad, shift_grad, head_grad, chead_grad = done
     return (

time: 163 us -> 156 us (0.957)
  Pallas kernels: 157 us -> 153 us
  local copies, waits for them, and re-layouts: 3.43 us -> 0 us
    pallas_call x1, Pallas kernels: 154 us -> 149 us  [per_device(): pl.pallas_call(functools.partial(kernel, scale, near_count, far_count), o...]
    unnamed x6 -> x0, local copies, waits for them, and re-layouts: 3.43 us -> none
    pallas_call x1, Pallas kernels: 2.32 us -> 4.08 us  [per_device(): pl.pallas_call(functools.partial(finish_kernel, scale), out_shape=(jax.Sh...]
where the time goes in v4:
time: 156 us
  Pallas kernels  153 us (98%)
  between operations  2.42 us (2%)
    pallas_call x1, Pallas kernels, per_device(): pl.pallas_call(functools.partial(kernel, scale, near_count, far_count), o...  149 us
    pallas_call x1, Pallas kernels, per_device(): pl.pallas_call(functools.partial(finish_kernel, scale), out_shape=(jax.Sh...  4.08 us

profile of v4, /device:TPU:0, one launch (start us, length us, event | category | flops | bytes accessed | tf_op | source)
XLA Modules:
  0.0 155.9 jit_solution(16798556110760956468)
XLA Ops:
  0.6 149.3 %shard_map.213 = (f32[768,256]{1,0:T(8,128)}, bf16[2,3,4,320,128]{4,3,2,1,0:T(8,128)(2,1)}, bf16[2,64,128]{2,1,0:T(8,128)(2,1)}, f32[1,1]{1,0:T(1,128)}, bf16[2,2,15,256,768]{4,3,2,1,0:T(8,128)(2,1)}) custom-call(bf16[3072,256]{1,0:T(8,128)(2,1)} %latent.1, s32[1,3072]{1,0:T(1,128)} %bitcast.14, s32[5,3072]{1,0:T(8,128)} %actions_in.1, ...), custom_call_target="tpu_custom_call" | custom-call | tf_op jit(solution)/shard_map/pallas_call | solution.py:1088
  150.0 4.1 %shard_map.214 = (f32[768,1,256]{2,1,0:T(1,128)}, f32[1,2,256,256]{3,2,1,0:T(8,128)}, f32[1,2,2,2,256,256]{5,4,3,2,1,0:T(8,128)}, f32[1,4,256]{2,1,0:T(4,128)}, ...) custom-call(f32[768,256]{1,0:T(8,128)} %get-tuple-element.23.latent_, ...), custom_call_target="tpu_custom_call" | custom-call | tf_op jit(solution)/shard_map/pallas_call | solution.py:1109

commit v5 on v4

--- a/solution.py
+++ b/solution.py
@@ -28,10 +28,12 @@
     )
 
 
-def gelu_pair(half):
+def gelu_pair(half, short):
     inner = half * (half * half * K2 + K1)
     plus = jnp.tanh(inner) + 1.0
     out = half * plus
+    if short:
+        half, inner, plus = half.astype(BF16), inner.astype(BF16), plus.astype(BF16)
     slope = inner * 3.0 - half * (2.0 * K1)
     return out, (plus * ((2.0 - plus) * slope + 1.0)).astype(BF16)
 
@@ -335,7 +337,7 @@
                 half = unit * gain_of(n, band) + shift_of(n, band)
                 if n > 0 and n % 2 == 0:
                     half = half + 0.5 * resid[band, sub]
-                out, slope = gelu_pair(half)
+                out, slope = gelu_pair(half, n % 2 == 1)
                 if n == 0 or n == 2:
                     resid[band, sub] = out
                 if n == 4:

time: 156 us -> 155 us (level)
  no operation moved by 1% of the time
where the time goes in v5:
time: 155 us
  Pallas kernels  152 us (98%)
  between operations  2.42 us (2%)
    pallas_call x1, Pallas kernels, per_device(): pl.pallas_call(functools.partial(kernel, scale, near_count, far_count), o...  148 us
    pallas_call x1, Pallas kernels, per_device(): pl.pallas_call(functools.partial(finish_kernel, scale), out_shape=(jax.Sh...  4.08 us

profile of v5, /device:TPU:0, one launch (start us, length us, event | category | flops | bytes accessed | tf_op | source)
XLA Modules:
  0.0 154.7 jit_solution(8362213838723224860)
XLA Ops:
  0.6 148.2 %shard_map.213 = (f32[768,256]{1,0:T(8,128)}, bf16[2,3,4,320,128]{4,3,2,1,0:T(8,128)(2,1)}, bf16[2,64,128]{2,1,0:T(8,128)(2,1)}, f32[1,1]{1,0:T(1,128)}, bf16[2,2,15,256,768]{4,3,2,1,0:T(8,128)(2,1)}) custom-call(bf16[3072,256]{1,0:T(8,128)(2,1)} %latent.1, s32[1,3072]{1,0:T(1,128)} %bitcast.14, s32[5,3072]{1,0:T(8,128)} %actions_in.1, ...), custom_call_target="tpu_custom_call" | custom-call | tf_op jit(solution)/shard_map/pallas_call | solution.py:1090
  148.8 4.1 %shard_map.214 = (f32[768,1,256]{2,1,0:T(1,128)}, f32[1,2,256,256]{3,2,1,0:T(8,128)}, f32[1,2,2,2,256,256]{5,4,3,2,1,0:T(8,128)}, f32[1,4,256]{2,1,0:T(4,128)}, ...) custom-call(f32[768,256]{1,0:T(8,128)} %get-tuple-element.23.latent_, ...), custom_call_target="tpu_custom_call" | custom-call | tf_op jit(solution)/shard_map/pallas_call | solution.py:1111
